TPU v7x, 512 devices: a whole 4x4x16 slice. The times are simulated.
512 devices in a mesh: batch: 16 (over z), item: 32 (over x, y, core).
Axes of the slice: x: 4, y: 4, z: 16, core: 2. Of those that a mesh axis runs over, the one named last changes fastest.
Arguments:
- item_feat: bfloat16 [262144, 768], P(('batch', 'item')), may hold values from -6 to 6
- item_latent: bfloat16 [262144, 64], P(('batch', 'item')), may hold values from -1.5 to 1.5
- item_bias: bfloat16 [262144], P(('batch', 'item')), may hold values from -3 to 3
- projection: bfloat16 [768, 64], replicated, may hold values from -0.21875 to 0.21875
- user_factors: bfloat16 [131072, 128], P(('batch', 'item')), may hold values from -1.5 to 1.5
- user_ids: int32 [1048576], P(('batch', 'item')), may hold values from 0 to 255
- requests: int32 [16, 32, 32, 64], P('batch', 'item'), may hold values from 0 to 511, as said below
- pos_slot: int32 [1048576], P(('batch', 'item')), may hold values from 0 to 2047, as said below
- neg_slot: int32 [1048576], P(('batch', 'item')), may hold values from 0 to 2047, as said below
Outputs:
- item_latent_grad: float32 [262144, 64], P(('batch', 'item'))
- item_bias_grad: float32 [262144], P(('batch', 'item'))
- user_grad: float32 [131072, 128], P(('batch', 'item'))
- projection_grad: float32 [768, 64], replicated
Inputs may be any that keep to these rules, and one draw needn't show every extreme that they name: `requests`: within one device and one owner the 64 rows are distinct. Every slot holds a row; the triples of a device name only some of its slots. `pos_slot`: names a slot of the triple's device; low slots and low owners are named far more often. `neg_slot`: names a slot of the triple's device.
All inputs are finite; a program needn't handle non-finite values.
Results may differ from a plain program's by a relative error of at most 0.008.
Values may be sent and summed in bfloat16 or wider, within the bound.
No kernel may reach another device: no remote copies, remote signals or barrier semaphores. Data moves between devices by JAX's collectives and lax.ppermute only.
A program may use at most 64 MiB of HBM per device.

v0:
```python
import math

import jax
import jax.numpy as jnp
from jax import lax
from jax.sharding import PartitionSpec as P


def on_device(
    item_feat,
    item_latent,
    item_bias,
    projection,
    user_factors,
    user_ids,
    requests,
    pos_slot,
    neg_slot,
):
    owners = lax.axis_size("item")
    width = item_latent.shape[1]
    feats = item_feat.shape[1]
    table_rows = item_feat.shape[0]
    asked = lax.all_to_all(
        requests.reshape(owners, -1), "item", split_axis=0, concat_axis=0, tiled=True
    )
    capacity = asked.shape[1]
    rows = asked.reshape(-1)
    feat_rows = jnp.take(item_feat, rows, axis=0)
    lat_rows = jnp.take(item_latent, rows, axis=0).reshape(owners, capacity, width)
    bias_rows = jnp.take(item_bias, rows, axis=0).reshape(owners, capacity)
    got_feat, got_lat, got_bias = (
        lax.all_to_all(
            feat_rows.reshape(owners, capacity, feats),
            "item",
            split_axis=0,
            concat_axis=0,
            tiled=True,
        ),
        lax.all_to_all(lat_rows, "item", split_axis=0, concat_axis=0, tiled=True),
        lax.all_to_all(bias_rows, "item", split_axis=0, concat_axis=0, tiled=True),
    )
    got_feat = got_feat.reshape(-1, feats)
    visual = jnp.dot(got_feat, projection, preferred_element_type=jnp.float32).astype(jnp.bfloat16)
    slot_lat = got_lat.reshape(-1, width).astype(jnp.float32)
    slot_vis = visual.astype(jnp.float32)
    slot_bias = got_bias.reshape(-1).astype(jnp.float32)
    slots = slot_lat.shape[0]
    user_rows = jnp.take(user_factors, user_ids, axis=0).astype(jnp.float32)
    delta_lat = jnp.take(slot_lat, pos_slot, axis=0) - jnp.take(slot_lat, neg_slot, axis=0)
    delta_vis = jnp.take(slot_vis, pos_slot, axis=0) - jnp.take(slot_vis, neg_slot, axis=0)
    score = jnp.sum(user_rows[:, :width] * delta_lat, 1) + jnp.sum(
        user_rows[:, width:] * delta_vis, 1
    )
    score = score + jnp.take(slot_bias, pos_slot) - jnp.take(slot_bias, neg_slot)
    slope = -jax.nn.sigmoid(-score)
    user_grad = jax.ops.segment_sum(
        jnp.concatenate([slope[:, None] * delta_lat, slope[:, None] * delta_vis], 1),
        user_ids,
        num_segments=user_factors.shape[0],
    )
    both_slots = jnp.concatenate([pos_slot, neg_slot], 0)
    values = slope[:, None] * user_rows
    combined = jax.ops.segment_sum(
        jnp.concatenate([values, -values], 0), both_slots, num_segments=slots
    )
    bias_slot = jax.ops.segment_sum(
        jnp.concatenate([slope, -slope], 0), both_slots, num_segments=slots
    )
    contract = (((0,), (0,)), ((), ()))
    back_lat, back_bias = (
        lax.all_to_all(
            combined[:, :width].reshape(owners, capacity, width),
            "item",
            split_axis=0,
            concat_axis=0,
            tiled=True,
        ),
        lax.all_to_all(
            bias_slot.reshape(owners, capacity), "item", split_axis=0, concat_axis=0, tiled=True
        ),
    )
    coef_b = combined[:, width:].astype(jnp.bfloat16)
    local_term = lax.dot_general(got_feat, coef_b, contract, preferred_element_type=jnp.float32)
    item_latent_grad = jax.ops.segment_sum(
        back_lat.reshape(-1, width), rows, num_segments=table_rows
    )
    item_bias_grad = jax.ops.segment_sum(back_bias.reshape(-1), rows, num_segments=table_rows)
    total = pos_slot.shape[0] * lax.axis_size("batch") * owners
    projection_grad = lax.psum(local_term, ("batch", "item")) / math.sqrt(total)
    return (item_latent_grad, item_bias_grad, user_grad, projection_grad)


def solution(mesh):
    placed = (
        P(("batch", "item"), None),
        P(("batch", "item"), None),
        P(("batch", "item")),
        P(),
        P(("batch", "item"), None),
        P(("batch", "item")),
        P("batch", "item", None, None),
        P(("batch", "item")),
        P(("batch", "item")),
    )
    return jax.shard_map(
        on_device,
        mesh=mesh,
        in_specs=placed,
        out_specs=(
            P(("batch", "item"), None),
            P(("batch", "item")),
            P(("batch", "item"), None),
            P(),
        ),
        check_vma=False,
    )
```

profile of v0, /device:TPU:1, one launch (start us, length us, event | category | flops | bytes accessed | tf_op | source)
XLA Modules:
  0.0 697.4 jit_solution(11702216571753635758)
XLA Ops:
  7.2 10.5 %all-to-all-start = ((s32[32,1,64]{2,1,0:T(1,128)}), s32[32,1,64]{2,1,0:T(1,128)S(1)}, u32[]{:S(2)}, u32[]{:S(2)}) async-start(s32[32,1,64]{2,1,0:T(1,128)} %bitcast.27), calls=%async_computation | async-start | bytes 32768 | tf_op jit(solution)/shard_map/all_to_all | solution.py:24
  18.7 6.0 all-to-all-done
  24.8 13.1 %gather_fusion.3 = bf16[2048]{0:T(1024)(128)(2,1)S(1)} fusion(bf16[512]{0:T(512)(128)(2,1)S(1)} %copy-done.1, s32[2048]{0:T(1024)S(1)} %broadcast_clamp_fusion), kind=kCustom, calls=%fused_computation.9 | custom fusion | bytes 16384 | tf_op jit(solution)/shard_map/jit(_take)/gather | solution.py:31
  42.8 6.2 gather_fusion.1
  50.4 9.4 %gather_fusion.2 = bf16[2048,768]{1,0:T(8,128)(2,1)} fusion(bf16[512,768]{1,0:T(8,128)(2,1)S(1)} %copy-done, s32[2048]{0:T(1024)S(1)} %broadcast_clamp_fusion), kind=kCustom, calls=%fused_computation.8 | custom fusion | bytes 6299648 | tf_op jit(solution)/shard_map/jit(_take)/gather | solution.py:29
  59.8 7.5 %all-to-all-start.1 = ((bf16[32,2,2048]{2,1,0:T(2,128)(2,1)}), bf16[32,2,2048]{2,1,0:T(2,128)(2,1)S(1)}, u32[]{:S(2)}, u32[]{:S(2)}) async-start(bf16[32,2,2048]{2,1,0:T(2,128)(2,1)} %reshape.297), calls=%async_computation.1 | async-start | bytes 524288 | tf_op jit(solution)/shard_map/all_to_all | solution.py:40
  70.6 5.6 all-to-all-done.1
  76.3 4.6 all-to-all-start.2
  80.9 6.2 gather_fusion
  89.6 11.8 %gather_fusion.8 = f32[2048]{0:T(1024)S(1)} fusion(f32[2048]{0:T(1024)S(1)} %reshape.116, s32[2048]{0:T(1024)S(1)} %get-tuple-element.26), kind=kCustom, calls=%fused_computation.1.clone | custom fusion | bytes 24576 | tf_op jit(solution)/shard_map/jit(_take)/gather | solution.py:55
  101.4 11.8 %gather_fusion.9 = f32[2048]{0:T(1024)S(1)} fusion(f32[2048]{0:T(1024)S(1)} %reshape.116, s32[2048]{0:T(1024)S(1)} %get-tuple-element.28), kind=kCustom, calls=%fused_computation.5.clone | custom fusion | bytes 24576 | tf_op jit(solution)/shard_map/jit(_take)/gather | solution.py:55
  115.5 7.6 %gather_fusion.5 = f32[2048,64]{1,0:T(8,128)} fusion(f32[2048,64]{1,0:T(8,128)S(1)} %bitcast_convert_fusion, s32[2048]{0:T(1024)S(1)} %get-tuple-element.28), kind=kCustom, calls=%fused_computation.2.clone | custom fusion | bytes 1056768 | tf_op jit(solution)/shard_map/jit(_take)/gather | solution.py:50
  123.0 7.6 %gather_fusion.4 = f32[2048,64]{1,0:T(8,128)} fusion(f32[2048,64]{1,0:T(8,128)S(1)} %bitcast_convert_fusion, s32[2048]{0:T(1024)S(1)} %get-tuple-element.26), kind=kCustom, calls=%fused_computation.clone | custom fusion | bytes 1056768 | tf_op jit(solution)/shard_map/jit(_take)/gather | solution.py:50
  135.7 7.5 %gather_fusion.7 = f32[2048,64]{1,0:T(8,128)} fusion(f32[2048,64]{1,0:T(8,128)S(1)} %copy.25, s32[2048]{0:T(1024)S(1)} %get-tuple-element.28), kind=kCustom, calls=%fused_computation.4.clone | custom fusion | bytes 1056768 | tf_op jit(solution)/shard_map/jit(_take)/gather | solution.py:51
  143.3 7.6 %gather_fusion.6 = f32[2048,64]{1,0:T(8,128)} fusion(f32[2048,64]{1,0:T(8,128)S(1)} %copy.25, s32[2048]{0:T(1024)S(1)} %get-tuple-element.26), kind=kCustom, calls=%fused_computation.3.clone | custom fusion | bytes 1056768 | tf_op jit(solution)/shard_map/jit(_take)/gather | solution.py:51
  155.5 23.6 %scatter_custom_fusion.2 = f32[2048]{0:T(1024)S(1)} fusion(s32[4096]{0:T(1024)} %copy-done.10, f32[4096]{0:T(1024)S(1)} %pad_maximum_fusion, f32[]{:T(128)} %constant.57.clone.1), kind=kCustom, calls=%fused_computation.68 | custom fusion | flops 4096 | bytes 8704 | tf_op jit(solution)/shard_map/scatter-add | solution.py:67
  179.8 7.7 %all-to-all-start.5 = ((f32[32,1,64]{2,1,0:T(1,128)}), f32[32,1,64]{2,1,0:T(1,128)S(1)}, u32[]{:S(2)}, u32[]{:S(2)}) async-start(f32[32,1,64]{2,1,0:T(1,128)} %all_to_all.31), calls=%async_computation.5 | async-start | bytes 32768 | tf_op jit(solution)/shard_map/all_to_all | solution.py:79
  187.8 23.5 %scatter_custom_fusion = f32[2048,128]{1,0:T(8,128)S(1)} fusion(s32[4096]{0:T(1024)} %copy-done.10, f32[2048,128]{1,0:T(8,128)} %get-tuple-element.23, f32[]{:T(128)} %constant.96, f32[2048,128]{1,0:T(8,128)S(1)} %get-tuple-element.22, f32[]{:T(128)} %constant.57.clone.1), kind=kCustom, calls=%fused_computation.18 | custom fusion | flops 1048576 | bytes 3146752 | tf_op jit(solution)/shard_map/scatter-add | solution.py:64
  216.3 7.4 %all-to-all-start.4 = ((f32[32,1,4096]{2,1,0:T(1,128)}), f32[32,1,4096]{2,1,0:T(1,128)S(1)}, u32[]{:S(2)}, u32[]{:S(2)}) async-start(f32[32,1,4096]{2,1,0:T(1,128)} %reshape.299), calls=%async_computation.4 | async-start | bytes 1048576 | tf_op jit(solution)/shard_map/all_to_all | solution.py:72
  223.7 4.5 broadcast_multiply_fusion.1
  228.2 13.0 %scatter_custom_fusion.4 = f32[256,128]{1,0:T(8,128)} fusion(s32[2048]{0:T(1024)S(1)} %copy-done.7, f32[2048,64]{1,0:T(8,128)} %get-tuple-element.25, f32[]{:T(128)} %constant.96, f32[2048,64]{1,0:T(8,128)S(1)} %get-tuple-element.24, f32[]{:T(128)} %constant.57.clone.1), kind=kCustom, calls=%fused_computation.27 | custom fusion | flops 524288 | bytes 1703944 | tf_op jit(solution)/shard_map/scatter-add | solution.py:57
  242.5 15.4 %scatter_custom_fusion.3 = f32[512]{0:T(512)} fusion(s32[2048]{0:T(1024)} %reshape.207, f32[2048]{0:T(1024)S(1)} %reshape.225, f32[]{:T(128)} %constant.57.clone.1), kind=kCustom, calls=%fused_computation.71 | custom fusion | flops 2048 | bytes 2560 | tf_op jit(solution)/shard_map/scatter-add | solution.py:88
  257.8 415.9 %all-reduce.2.cloned.1.call-done = f32[768,64]{0,1:T(8,128)} async-done(((f32[768,64]{0,1:T(8,128)}), f32[768,64]{0,1:T(8,128)}) %all-reduce.2.cloned.1.call-update) | async-done | bytes 196624 | tf_op jit(solution)/shard_map/psum | solution.py:90
  678.2 11.7 %scatter_custom_fusion.1 = f32[512,64]{1,0:T(8,128)S(1)} fusion(s32[2048]{0:T(1024)} %reshape.207, f32[2048,64]{1,0:T(8,128)S(1)} %bitcast.22, f32[]{:T(128)} %constant.57.clone.1), kind=kCustom, calls=%fused_computation.41 | custom fusion | flops 131072 | bytes 131584 | tf_op jit(solution)/shard_map/scatter-add | solution.py:85
  (70 shorter events, 37.5 us)
Async XLA Ops:
  7.2 43.2 %copy-start = (bf16[512,768]{1,0:T(8,128)(2,1)S(1)}, bf16[512,768]{1,0:T(8,128)(2,1)}, u32[]{:S(2)}) copy-start(bf16[512,768]{1,0:T(8,128)(2,1)} %param.13) | copy-start | bytes 2359300
  7.2 17.6 %copy-start.1 = (bf16[512]{0:T(512)(128)(2,1)S(1)}, bf16[512]{0:T(512)(128)(2,1)}, u32[]{:S(2)}) copy-start(bf16[512]{0:T(512)(128)(2,1)} %param.15) | copy-start | bytes 3076
  7.2 17.5 %all-to-all-start = ((s32[32,1,64]{2,1,0:T(1,128)}), s32[32,1,64]{2,1,0:T(1,128)S(1)}, u32[]{:S(2)}, u32[]{:S(2)}) async-start(s32[32,1,64]{2,1,0:T(1,128)} %bitcast.27), calls=%async_computation | async-start | bytes 32768 | tf_op jit(solution)/shard_map/all_to_all | solution.py:24
  38.6 21.2 %all-to-all-start.3 = ((bf16[32,1,64]{2,1,0:T(2,128)(2,1)}), bf16[32,1,64]{2,1,0:T(2,128)(2,1)S(1)}, u32[]{:S(2)}, u32[]{:S(2)}) async-start(bf16[32,1,64]{2,1,0:T(2,128)(2,1)} %copy.30), calls=%async_computation.3 | async-start | bytes 32768 | tf_op jit(solution)/shard_map/all_to_all | solution.py:41
  59.8 16.5 %all-to-all-start.1 = ((bf16[32,2,2048]{2,1,0:T(2,128)(2,1)}), bf16[32,2,2048]{2,1,0:T(2,128)(2,1)S(1)}, u32[]{:S(2)}, u32[]{:S(2)}) async-start(bf16[32,2,2048]{2,1,0:T(2,128)(2,1)} %reshape.297), calls=%async_computation.1 | async-start | bytes 524288 | tf_op jit(solution)/shard_map/all_to_all | solution.py:40
  70.6 10.3 %copy-start.7 = (s32[2048]{0:T(1024)S(1)}, s32[2048]{0:T(1024)}, u32[]{:S(2)}) copy-start(s32[2048]{0:T(1024)} %param.18) | copy-start | bytes 24580
  70.6 10.3 %copy-start.2 = (bf16[256,128]{1,0:T(8,128)(2,1)S(1)}, bf16[256,128]{1,0:T(8,128)(2,1)}, u32[]{:S(2)}) copy-start(bf16[256,128]{1,0:T(8,128)(2,1)} %param.17) | copy-start | bytes 196612
  76.3 54.3 %all-to-all-start.2 = ((bf16[32,64,768]{2,1,0:T(8,128)(2,1)}), bf16[32,64,768]{2,1,0:T(8,128)(2,1)}, u32[]{:S(2)}, u32[]{:S(2)}) async-start(bf16[32,64,768]{2,1,0:T(8,128)(2,1)} %broadcast_select_fusion), calls=%async_computation.2 | async-start | bytes 6291456 | tf_op jit(solution)/shard_map/all_to_all | solution.py:33
  80.9 6.3 copy-start.5
  80.9 6.3 copy-start.6
  87.2 2.3 copy-start.8
  87.2 14.1 %copy-start.10 = (s32[4096]{0:T(1024)}, s32[4096]{0:T(1024)S(1)}, u32[]{:S(2)}) copy-start(s32[4096]{0:T(1024)S(1)} %get-tuple-element.29) | copy-start | bytes 49156
  123.0 7.6 %copy-start.4 = (bf16[768,64]{0,1:T(8,128)(2,1)S(1)}, bf16[768,64]{0,1:T(8,128)(2,1)}, u32[]{:S(2)}) copy-start(bf16[768,64]{0,1:T(8,128)(2,1)} %param.16) | copy-start | bytes 294916
  150.9 3.1 copy-start.9
  179.8 36.4 %all-to-all-start.5 = ((f32[32,1,64]{2,1,0:T(1,128)}), f32[32,1,64]{2,1,0:T(1,128)S(1)}, u32[]{:S(2)}, u32[]{:S(2)}) async-start(f32[32,1,64]{2,1,0:T(1,128)} %all_to_all.31), calls=%async_computation.5 | async-start | bytes 32768 | tf_op jit(solution)/shard_map/all_to_all | solution.py:79
  187.5 486.2 %all-reduce.2.cloned.1.call-start = ((), (), s32[]{:S(2)}) async-start(), calls=%async_computation.6 | async-start | bytes 393216 | tf_op jit(solution)/shard_map/psum | solution.py:90
  211.3 12.4 %copy-start.3 = (f32[2048,64]{1,0:T(8,128)S(1)}, f32[2048,64]{1,0:T(8,128)}, u32[]{:S(2)}) copy-start(f32[2048,64]{1,0:T(8,128)} %gather_fusion.5) | copy-start | bytes 1572868
  216.3 459.1 %all-to-all-start.4 = ((f32[32,1,4096]{2,1,0:T(1,128)}), f32[32,1,4096]{2,1,0:T(1,128)S(1)}, u32[]{:S(2)}, u32[]{:S(2)}) async-start(f32[32,1,4096]{2,1,0:T(1,128)} %reshape.299), calls=%async_computation.4 | async-start | bytes 1048576 | tf_op jit(solution)/shard_map/all_to_all | solution.py:72
Sparse Core Ops, SparseCore 0:
  216.4 457.2 all-reduce.1
where the time goes:
time: 698 us; the launch traced here: 697 us
  waiting for transfers between devices  428 us (61%)
  other arithmetic  106 us (15%)
  local copies, waits for them, and re-layouts  99.8 us (14%)
  starting transfers between devices  42 us (6%)
  between operations  14.4 us (2%)
  matrix products  7.21 us (1%)
    psum x1, waiting for transfers between devices, on_device(): projection_grad = lax.psum(local_term, ('batch', 'item')) / math.sqrt(total)  416 us
    scatter-add x1, other arithmetic, on_device(): jax.ops.segment_sum(jnp.concatenate([slope, -slope], 0), both_slots, num_...  23.6 us
    scatter-add x1, other arithmetic, on_device(): jax.ops.segment_sum(jnp.concatenate([values, -values], 0), both_slots, nu...  23.5 us
    scatter-add x1, other arithmetic, on_device(): jax.ops.segment_sum(back_bias.reshape(-1), rows, num_segments=table_rows)  15.4 us
  transfers between devices with their start and end apart: 7, of which 3 were waited for; matrix products, arithmetic and copies ran while one was open for 19% of the time, Pallas kernels for 0%

commit v1 on v0

v1 whole, which is shorter than its diff:
```python
import functools
import math

import jax
import jax.numpy as jnp
from jax import lax
from jax.experimental import pallas as pl
from jax.experimental.pallas import tpu as pltpu
from jax.sharding import PartitionSpec as P

BF = jnp.bfloat16
F32 = jnp.float32
VM = pl.BlockSpec(memory_space=pltpu.VMEM)
NN = (((1,), (0,)), ((), ()))
NT = (((1,), (1,)), ((), ()))
MIB = 1024 * 1024


def mm(a, b, dims=NN):
    return lax.dot_general(a, b, dims, preferred_element_type=F32)


def split(x):
    hi = x.astype(BF)
    return hi, (x - hi.astype(F32)).astype(BF)


def one_hot(rows, index):
    n = index.shape[1]
    return (lax.broadcasted_iota(jnp.int32, (rows, n), 0) == index).astype(F32)


def lane_index(ref, first, count):
    return jnp.concatenate([ref[r : r + 1, :] for r in range(first, first + count)], axis=1)


def pack(out_ref, owner, block, width, cap):
    lat, vis, bias = block[:width], block[width : 2 * width], block[2 * width : 2 * width + 8]
    out_ref[owner, 0:width, :] = jnp.concatenate([lat, vis], axis=1).astype(BF)
    out_ref[owner, width : width + 8, :] = jnp.concatenate(
        [bias, jnp.zeros((8, cap), F32)], axis=1
    ).astype(BF)


def unpack(in_ref, flat_ref, width, cap):
    owners = in_ref.shape[0]
    for o in range(0, owners, 2):
        a, b = in_ref[o].astype(F32), in_ref[o + 1].astype(F32)
        cols = slice(o * cap, (o + 2) * cap)
        lat = jnp.concatenate([a[:width, :cap], b[:width, :cap]], axis=1)
        vis = jnp.concatenate([a[:width, cap:], b[:width, cap:]], axis=1)
        bias = jnp.concatenate([a[width:, :cap], b[width:, :cap]], axis=1)
        flat_ref[0:width, cols] = lat.astype(BF)
        flat_ref[width : 2 * width, cols] = vis.astype(BF)
        flat_ref[2 * width :, cols] = jnp.concatenate(
            [bias, jnp.zeros((8, 2 * cap), F32)], axis=0
        ).astype(BF)


def table_kernel(feat_ref, lat_ref, bias_ref, proj_ref, out_ref):
    width, rows = lat_ref.shape
    out_ref[0:width, :] = lat_ref[...]
    out_ref[width : 2 * width, :] = mm(proj_ref[...], feat_ref[...], NT).astype(BF)
    first = lax.broadcasted_iota(jnp.int32, (16, rows), 0) == 0
    bias = jnp.where(first, bias_ref[...].astype(F32), 0.0)
    out_ref[2 * width :, :] = bias.astype(BF)


def send_kernel(table_ref, asked_ref, out_ref):
    owners, cap = asked_ref.shape
    rows = table_ref.shape[1]
    width = (table_ref.shape[0] - 16) // 2
    table = table_ref[...]
    for o in range(0, owners, 4):
        hot = one_hot(rows, lane_index(asked_ref, o, 4)).astype(BF)
        got = mm(table, hot)
        for k in range(4):
            pack(out_ref, o + k, got[:, k * cap : (k + 1) * cap], width, cap)


def user_kernel(user_ref, uid_ref, out_ref):
    users, width2 = user_ref.shape
    table = jnp.transpose(user_ref[...].astype(F32)).astype(BF)
    step = uid_ref.shape[1]
    for r in range(0, uid_ref.shape[0], 2):
        hot = one_hot(users, lane_index(uid_ref, r, 2)).astype(BF)
        out_ref[:, r * step : (r + 2) * step] = mm(table, hot).astype(BF)


def triple_kernel(
    got_ref, user_ref, pos_ref, neg_ref, uid_ref, send_ref, ugrad_ref, flat, diff, grad, ugd, *, users
):
    owners, cap = got_ref.shape[0], got_ref.shape[2] // 2
    width = got_ref.shape[1] - 8
    slots = owners * cap
    w2 = 2 * width
    unpack(got_ref, flat, width, cap)
    step = 2 * pos_ref.shape[1]
    table = flat[...]
    for r in range(0, pos_ref.shape[0], 2):
        cols = slice(r // 2 * step, (r // 2 + 1) * step)
        d = one_hot(slots, lane_index(pos_ref, r, 2)) - one_hot(slots, lane_index(neg_ref, r, 2))
        d = d.astype(BF)
        diff[:, cols] = d
        delta = mm(table, d)
        u = user_ref[:, cols].astype(F32)
        x = jnp.sum(u * delta[:w2], axis=0, keepdims=True) + delta[w2 : w2 + 1]
        g = -jax.nn.sigmoid(-x)
        hi, lo = split(g * u)
        first = lax.broadcasted_iota(jnp.int32, (16, step), 0) == 0
        bhi, blo = split(jnp.where(first, g, 0.0))
        grad[0:w2, cols] = hi
        grad[w2 : w2 + 16, cols] = bhi
        grad[w2 + 16 : 2 * w2 + 16, cols] = lo
        grad[2 * w2 + 16 :, cols] = blo
        hi, lo = split(g * delta[:w2])
        ugd[0:w2, cols] = hi
        ugd[w2:, cols] = lo
    coef = grad[...]
    for o in range(0, owners, 4):
        both = mm(coef, diff[o * cap : (o + 4) * cap, :], NT)
        total = both[: w2 + 16] + both[w2 + 16 :]
        for k in range(4):
            pack(send_ref, o + k, total[:, k * cap : (k + 1) * cap], width, cap)
    hot = one_hot(users, lane_index(uid_ref, 0, uid_ref.shape[0])).astype(BF)
    both = mm(hot, ugd[...], NT)
    ugrad_ref[...] = both[:, :w2] + both[:, w2:]


def row_kernel(back_ref, asked_ref, feat_ref, lat_ref, bias_ref, term_ref, flat):
    owners, cap = asked_ref.shape
    width = back_ref.shape[1] - 8
    rows, feats = feat_ref.shape
    unpack(back_ref, flat, width, cap)
    hot = one_hot(rows, lane_index(asked_ref, 0, owners)).astype(BF)
    total = mm(flat[...], hot, NT)
    lat_ref[...] = total[:width]
    bias_ref[...] = total[2 * width : 2 * width + 1]
    hi, lo = split(total[width : 2 * width])
    both = mm(jnp.concatenate([hi, lo], axis=0), feat_ref[...])
    term = both[:width] + both[width:]
    across = feats // 128
    tiles = [(i, j) for i in range(width // 8) for j in range(across)]
    per = term_ref.shape[1] // 8
    for t in range(owners * per):
        o, k = divmod(t, per)
        if t < len(tiles):
            i, j = tiles[t]
            tile = term[8 * i : 8 * i + 8, 128 * j : 128 * j + 128]
        else:
            tile = jnp.zeros((8, 128), F32)
        term_ref[o, 8 * k : 8 * k + 8, :] = tile


def sum_kernel(in_ref, out_ref, *, scale):
    total = in_ref[0]
    for k in range(1, in_ref.shape[0]):
        total = total + in_ref[k]
    out_ref[...] = jnp.broadcast_to((total * scale)[None], out_ref.shape)


def join_kernel(in_ref, out_ref):
    across = out_ref.shape[1] // 128
    per = in_ref.shape[1] // 8
    for t in range(out_ref.shape[0] // 8 * across):
        i, j = divmod(t, across)
        o, k = divmod(t, per)
        out_ref[8 * i : 8 * i + 8, 128 * j : 128 * j + 128] = in_ref[o, 8 * k : 8 * k + 8, :]


def call(kernel, out, *args, scratch=(), limit=32, flops=0, moved=0):
    many = isinstance(out, (list, tuple))
    return pl.pallas_call(
        kernel,
        out_shape=out,
        in_specs=[VM] * len(args),
        out_specs=[VM] * len(out) if many else VM,
        scratch_shapes=list(scratch),
        compiler_params=pltpu.CompilerParams(vmem_limit_bytes=limit * MIB),
        cost_estimate=pl.CostEstimate(flops=flops, bytes_accessed=moved, transcendentals=0),
    )(*args)


def shape(dims, dtype):
    return jax.ShapeDtypeStruct(dims, dtype)


def exchange(x, axis):
    return lax.all_to_all(x, axis, split_axis=0, concat_axis=0, tiled=True)


def on_device(
    item_feat,
    item_latent,
    item_bias,
    projection,
    user_factors,
    user_ids,
    requests,
    pos_slot,
    neg_slot,
):
    owners = lax.axis_size("item")
    groups = lax.axis_size("batch")
    rows, feats = item_feat.shape
    width = item_latent.shape[1]
    users = user_factors.shape[0]
    cap = requests.shape[-1]
    slots = owners * cap
    triples = pos_slot.shape[0]
    w2 = 2 * width
    high = w2 + 16
    lines = triples // 128

    asked = exchange(requests.reshape(owners, cap), "item")
    table = call(
        table_kernel,
        shape((high, rows), BF),
        item_feat,
        item_latent.T,
        item_bias.reshape(1, rows),
        projection.T,
        flops=2 * rows * feats * width,
        moved=2 * rows * (feats + high),
    )
    pos = pos_slot.reshape(lines, 128)
    neg = neg_slot.reshape(lines, 128)
    uid = user_ids.reshape(lines, 128)
    user_rows = call(
        user_kernel,
        shape((w2, triples), BF),
        user_factors,
        uid,
        flops=2 * users * w2 * triples,
        moved=4 * w2 * triples,
    )
    message = shape((owners, width + 8, 2 * cap), BF)
    sent = call(send_kernel, message, table, asked, flops=2 * rows * slots * high)
    got = exchange(sent, "item")
    back, user_grad = call(
        functools.partial(triple_kernel, users=users),
        [message, shape((users, w2), F32)],
        got,
        user_rows,
        pos,
        neg,
        uid,
        scratch=[
            pltpu.VMEM((high, slots), BF),
            pltpu.VMEM((slots, triples), BF),
            pltpu.VMEM((2 * high, triples), BF),
            pltpu.VMEM((2 * w2, triples), BF),
        ],
        limit=40,
        flops=6 * slots * triples * high,
    )
    returned = exchange(back, "item")
    tiles = width // 8 * (feats // 128)
    chunk = -(-tiles // owners) * 8
    lat_grad, bias_grad, term = call(
        row_kernel,
        [shape((width, rows), F32), shape((1, rows), F32), shape((owners, chunk, 128), F32)],
        returned,
        asked,
        item_feat,
        scratch=[pltpu.VMEM((high, slots), BF)],
        flops=2 * rows * slots * high,
    )
    total = triples * groups * owners
    parts = exchange(term, "item")
    group_sum = call(
        functools.partial(sum_kernel, scale=1.0), shape((groups, chunk, 128), F32), parts
    )
    parts = exchange(group_sum, "batch")
    whole = call(
        functools.partial(sum_kernel, scale=1.0 / math.sqrt(total)),
        shape((owners, chunk, 128), F32),
        parts,
    )
    parts = exchange(whole, "item")
    projection_grad = call(join_kernel, shape((width, feats), F32), parts)
    return (lat_grad.T, bias_grad.reshape(rows), user_grad, projection_grad.T)


def solution(mesh):
    placed = (
        P(("batch", "item"), None),
        P(("batch", "item"), None),
        P(("batch", "item")),
        P(),
        P(("batch", "item"), None),
        P(("batch", "item")),
        P("batch", "item", None, None),
        P(("batch", "item")),
        P(("batch", "item")),
    )
    return jax.shard_map(
        on_device,
        mesh=mesh,
        in_specs=placed,
        out_specs=(
            P(("batch", "item"), None),
            P(("batch", "item")),
            P(("batch", "item"), None),
            P(),
        ),
        check_vma=False,
    )
```

time: 698 us -> 116 us (0.17)
  waiting for transfers between devices: 428 us -> 15.7 us
  other arithmetic: 106 us -> 0 us
  local copies, waits for them, and re-layouts: 99.8 us -> 2.89 us
  blocking collectives: 0 us -> 68.4 us
  starting transfers between devices: 42 us -> 14.7 us
  between operations: 14.4 us -> 0.73 us
  Pallas kernels: 0 us -> 13 us
  matrix products: 7.21 us -> 0 us
    psum x1 -> x0, waiting for transfers between devices: 416 us -> none  [on_device(): projection_grad = lax.psum(local_term, ('batch', 'item')) / math.sqrt(total)]
    gather x11 -> x0, local copies, waits for them, and re-layouts: 88.7 us -> none  [the longest x2 13.2 us: on_device(): bias_rows = jnp.take(item_bias, rows, axis=0).reshape(owners, capacity)]
    scatter-add x5 -> x0, other arithmetic: 87.2 us -> none  [the longest x1 23.6 us: on_device(): jax.ops.segment_sum(jnp.concatenate([slope, -slope], 0), both_slots, num_...]
    all_to_all x0 -> x4, blocking collectives: none -> 68.4 us  [exchange(): return lax.all_to_all(x, axis, split_axis=0, concat_axis=0, tiled=True)]
    all_to_all x6 -> x2, starting transfers between devices: 41.8 us -> 14.7 us  [exchange(): return lax.all_to_all(x, axis, split_axis=0, concat_axis=0, tiled=True)]
    pallas_call x0 -> x8, Pallas kernels: none -> 13 us  [call(): pl.pallas_call(kernel, out_shape=out, in_specs=[VM] * len(args), out_spec...]
    dot_general x2 -> x0, matrix products: 7.21 us -> none  [the longest x1 3.74 us: on_device(): jnp.dot(got_feat, projection, preferred_element_type=jnp.float32)]
    all_to_all x6 -> x2, waiting for transfers between devices: 11.7 us -> 15.7 us  [exchange(): return lax.all_to_all(x, axis, split_axis=0, concat_axis=0, tiled=True)]
  transfers between devices with their start and end apart: 7 -> 2, of which waited for: 3 -> 2; matrix products, arithmetic and copies ran while one was open for 19% -> 0% of each run, Pallas kernels for 0% -> 1%
where the time goes in v1:
time: 116 us; the launch traced here: 115 us
  blocking collectives  68.4 us (59%)
  waiting for transfers between devices  15.7 us (14%)
  starting transfers between devices  14.7 us (13%)
  Pallas kernels  13 us (11%)
  local copies, waits for them, and re-layouts  2.89 us (2%)
    all_to_all x4, blocking collectives, exchange(): return lax.all_to_all(x, axis, split_axis=0, concat_axis=0, tiled=True)  68.4 us
    all_to_all x2, waiting for transfers between devices, exchange(): return lax.all_to_all(x, axis, split_axis=0, concat_axis=0, tiled=True)  15.7 us
    all_to_all x2, starting transfers between devices, exchange(): return lax.all_to_all(x, axis, split_axis=0, concat_axis=0, tiled=True)  14.7 us
    pallas_call x8, Pallas kernels, call(): pl.pallas_call(kernel, out_shape=out, in_specs=[VM] * len(args), out_spec...  13 us
    unnamed x18, local copies, waits for them, and re-layouts  2.89 us
  transfers between devices with their start and end apart: 2, of which 2 were waited for; matrix products, arithmetic and copies ran while one was open for 0% of the time, Pallas kernels for 1%

profile of v1, /device:TPU:1, one launch (start us, length us, event | category | flops | bytes accessed | tf_op | source)
XLA Modules:
  0.0 115.4 jit_solution(17426175999534645883)
XLA Ops:
  0.6 0.0 copy-start.8
  0.6 10.4 %all-to-all-start = ((s32[32,1,64]{2,1,0:T(1,128)}), s32[32,1,64]{2,1,0:T(1,128)S(1)}, u32[]{:S(2)}, u32[]{:S(2)}) async-start(s32[32,1,64]{2,1,0:T(1,128)} %bitcast.19), calls=%async_computation | async-start | bytes 32768 | tf_op jit(solution)/shard_map/all_to_all | solution.py:189
  11.0 0.0 copy-done.8
  11.0 0.0 copy-start
  11.1 1.1 copy-done
  12.2 0.9 copy-done.2
  13.1 0.8 copy-done.3
  13.9 0.4 shard_map.120.table_ref
  14.3 3.7 %all-to-all-done = s32[32,1,64]{2,1,0:T(1,128)S(1)} async-done(((s32[32,1,64]{2,1,0:T(1,128)}), s32[32,1,64]{2,1,0:T(1,128)S(1)}, u32[]{:S(2)}, u32[]{:S(2)}) %all-to-all-start) | async-done | bytes 8224 | tf_op jit(solution)/shard_map/all_to_all | solution.py:189
  18.0 1.5 %shard_map.121 = bf16[32,72,128]{2,1,0:T(8,128)(2,1)} custom-call(bf16[144,512]{1,0:T(8,128)(2,1)S(1)} %shard_map.120.table_ref, s32[32,64]{1,0:T(8,128)S(1)} %bitcast.11), custom_call_target="tpu_custom_call" | custom-call | flops 301989888 | tf_op jit(solution)/shard_map/pallas_call | solution.py:173
  19.5 4.3 %all-to-all-start.1 = ((bf16[32,72,128]{2,1,0:T(8,128)(2,1)}), bf16[32,72,128]{2,1,0:T(8,128)(2,1)S(1)}, u32[]{:S(2)}, u32[]{:S(2)}) async-start(bf16[32,72,128]{2,1,0:T(8,128)(2,1)} %shard_map.121), calls=%async_computation.1 | async-start | bytes 1179648 | tf_op jit(solution)/shard_map/all_to_all | solution.py:189
  23.9 0.0 copy-done.4
  23.9 0.0 copy-done.5
  23.9 0.0 copy-start.6
  23.9 0.0 copy-start.7
  23.9 0.4 shard_map.122.user_ref
  24.3 12.0 %all-to-all-done.1.got_ref = bf16[32,72,128]{2,1,0:T(8,128)(2,1)S(1)} async-done(((bf16[32,72,128]{2,1,0:T(8,128)(2,1)}), bf16[32,72,128]{2,1,0:T(8,128)(2,1)S(1)}, u32[]{:S(2)}, u32[]{:S(2)}) %all-to-all-start.1) | async-done | bytes 589856 | tf_op jit(solution)/shard_map/all_to_all | solution.py:189
  36.3 8.4 %shard_map.123 = (bf16[32,72,128]{2,1,0:T(8,128)(2,1)S(1)}, f32[256,128]{1,0:T(8,128)}) custom-call(bf16[32,72,128]{2,1,0:T(8,128)(2,1)S(1)} %all-to-all-done.1.got_ref, bf16[128,2048]{1,0:T(8,128)(2,1)S(1)} %shard_map.122.user_ref, s32[16,128]{1,0:T(8,128)S(1)} %bitcast.16, s32[16,128]{1,0:T(8,128)S(1)} %bitcast.17, s32[16,128]{1,0:T(8,128)S(1)} %bitcast.15), custom_call_target="tpu_custom_call" | custom-call | flops 3623878656 | tf_op jit(solution)/shard_map/pallas_call | solution.py:173
  44.7 15.8 %all_to_all.36.back_ref = bf16[32,72,128]{2,1,0:T(8,128)(2,1)S(1)} all-to-all(bf16[32,72,128]{2,1,0:T(8,128)(2,1)S(1)} %get-tuple-element.9), channel_id=1, replica_groups=mesh['batch'=16,'item'=32] {'item'}, dimensions={0} | all-to-all | bytes 1179648 | tf_op jit(solution)/shard_map/all_to_all | solution.py:189
  60.5 1.5 %shard_map.124 = (f32[64,512]{1,0:T(8,128)}, f32[1,512]{1,0:T(1,128)}, f32[32,16,128]{2,1,0:T(8,128)S(1)}) custom-call(bf16[32,72,128]{2,1,0:T(8,128)(2,1)S(1)} %all_to_all.36.back_ref, s32[32,64]{1,0:T(8,128)S(1)} %bitcast.12, bf16[512,768]{1,0:T(8,128)(2,1)S(1)} %copy-done.1), custom_call_target="tpu_custom_call" | custom-call | flops 301989888 | tf_op jit(solution)/shard_map/pallas_call | solution.py:173
  62.0 12.4 %all_to_all.37.in_ref = f32[32,16,128]{2,1,0:T(8,128)S(1)} all-to-all(f32[32,16,128]{2,1,0:T(8,128)S(1)} %get-tuple-element.13), channel_id=1, replica_groups=mesh['batch'=16,'item'=32] {'item'}, dimensions={0} | all-to-all | bytes 524288 | tf_op jit(solution)/shard_map/all_to_all | solution.py:189
  74.5 25.0 %all_to_all.38.in_ref = f32[16,16,128]{2,1,0:T(8,128)S(1)} all-to-all(f32[16,16,128]{2,1,0:T(8,128)S(1)} %shard_map.125), channel_id=1, replica_groups=mesh['batch'=16,'item'=32] {'batch'}, dimensions={0} | all-to-all | bytes 262144 | tf_op jit(solution)/shard_map/all_to_all | solution.py:189
  99.5 15.1 %all_to_all.39.in_ref = f32[32,16,128]{2,1,0:T(8,128)S(1)} all-to-all(f32[32,16,128]{2,1,0:T(8,128)S(1)} %shard_map.126), channel_id=1, replica_groups=mesh['batch'=16,'item'=32] {'item'}, dimensions={0} | all-to-all | bytes 524288 | tf_op jit(solution)/shard_map/all_to_all | solution.py:189
  114.7 0.7 shard_map.127
  (11 shorter events, 0.1 us)
Async XLA Ops:
  0.6 10.4 %copy-start.8 = (bf16[512]{0:T(512)(128)(2,1)S(1)}, bf16[512]{0:T(512)(128)(2,1)}, u32[]{:S(2)}) copy-start(bf16[512]{0:T(512)(128)(2,1)} %param.11) | copy-start | bytes 3076
  0.6 17.4 %all-to-all-start = ((s32[32,1,64]{2,1,0:T(1,128)}), s32[32,1,64]{2,1,0:T(1,128)S(1)}, u32[]{:S(2)}, u32[]{:S(2)}) async-start(s32[32,1,64]{2,1,0:T(1,128)} %bitcast.19), calls=%async_computation | async-start | bytes 32768 | tf_op jit(solution)/shard_map/all_to_all | solution.py:189
  11.0 1.1 copy-start
  12.2 0.9 copy-start.2
  13.1 0.8 copy-start.3
  19.5 4.3 %copy-start.4 = (bf16[256,128]{1,0:T(8,128)(2,1)S(1)}, bf16[256,128]{1,0:T(8,128)(2,1)}, u32[]{:S(2)}) copy-start(bf16[256,128]{1,0:T(8,128)(2,1)} %user_ref.1) | copy-start | bytes 196612
  19.5 4.4 %copy-start.5 = (s32[2048]{0:T(1024)S(1)}, s32[2048]{0:T(1024)}, u32[]{:S(2)}) copy-start(s32[2048]{0:T(1024)} %param.14) | copy-start | bytes 24580
  19.5 16.7 %all-to-all-start.1 = ((bf16[32,72,128]{2,1,0:T(8,128)(2,1)}), bf16[32,72,128]{2,1,0:T(8,128)(2,1)S(1)}, u32[]{:S(2)}, u32[]{:S(2)}) async-start(bf16[32,72,128]{2,1,0:T(8,128)(2,1)} %shard_map.121), calls=%async_computation.1 | async-start | bytes 1179648 | tf_op jit(solution)/shard_map/all_to_all | solution.py:189
  23.9 12.4 %copy-start.6 = (s32[2048]{0:T(1024)S(1)}, s32[2048]{0:T(1024)}, u32[]{:S(2)}) copy-start(s32[2048]{0:T(1024)} %param.16) | copy-start | bytes 24580
  23.9 12.4 %copy-start.7 = (s32[2048]{0:T(1024)S(1)}, s32[2048]{0:T(1024)}, u32[]{:S(2)}) copy-start(s32[2048]{0:T(1024)} %param.17) | copy-start | bytes 24580
  44.7 15.8 %copy-start.1 = (bf16[512,768]{1,0:T(8,128)(2,1)S(1)}, bf16[512,768]{1,0:T(8,128)(2,1)}, u32[]{:S(2)}) copy-start(bf16[512,768]{1,0:T(8,128)(2,1)} %feat_ref.3) | copy-start | bytes 2359300

commit v2 on v1

v2 whole, which is shorter than its diff:
```python
import functools
import math

import jax
import jax.numpy as jnp
from jax import lax
from jax.experimental import pallas as pl
from jax.experimental.pallas import tpu as pltpu
from jax.sharding import PartitionSpec as P

BF = jnp.bfloat16
F32 = jnp.float32
VM = pl.BlockSpec(memory_space=pltpu.VMEM)
NN = (((1,), (0,)), ((), ()))
NT = (((1,), (1,)), ((), ()))
MIB = 1024 * 1024


def mm(a, b, dims=NN):
    return lax.dot_general(a, b, dims, preferred_element_type=F32)


def split(x):
    hi = x.astype(BF)
    return hi, (x - hi.astype(F32)).astype(BF)


def matches(rows, index):
    shape16 = (16, index.shape[1])
    index = jnp.broadcast_to(index, shape16).astype(jnp.int16)
    line = lax.broadcasted_iota(jnp.int32, shape16, 0).astype(jnp.int16)
    return [line + jnp.int16(s) == index for s in range(0, rows, 16)]


def one_hot(rows, index):
    one, zero = jnp.ones((16, index.shape[1]), BF), jnp.zeros((16, index.shape[1]), BF)
    return jnp.concatenate([jnp.where(m, one, zero) for m in matches(rows, index)], axis=0)


def signed_hot(rows, plus, minus):
    same = plus == minus
    one, zero = jnp.ones((16, plus.shape[1]), BF), jnp.zeros((16, plus.shape[1]), BF)
    up = matches(rows, jnp.where(same, -1, plus))
    down = matches(rows, jnp.where(same, -1, minus))
    return jnp.concatenate(
        [jnp.where(p, one, jnp.where(m, -one, zero)) for p, m in zip(up, down)], axis=0
    )


def lane_index(ref, first, count):
    return jnp.concatenate([ref[r : r + 1, :] for r in range(first, first + count)], axis=1)


def fold(block):
    half = block.shape[0] // 2
    return jnp.concatenate([block[:half], block[half:]], axis=1)


def widen(block):
    return jnp.concatenate([block, jnp.zeros(block.shape, F32)], axis=1)


def pair(ref, o, lines, side, cap):
    cols = slice(side * cap, (side + 1) * cap)
    a, b = ref[o, lines, :].astype(F32), ref[o + 1, lines, :].astype(F32)
    return jnp.concatenate([a[:, cols], b[:, cols]], axis=1)


def table_kernel(feat_ref, lat_ref, bias_ref, proj_ref, out_ref):
    width, rows = lat_ref.shape
    out_ref[0:width, :] = lat_ref[...]
    out_ref[width : 2 * width, :] = mm(proj_ref[...], feat_ref[...], NT).astype(BF)
    first = lax.broadcasted_iota(jnp.int32, (16, rows), 0) == 0
    bias = jnp.where(first, bias_ref[...].astype(F32), 0.0)
    out_ref[2 * width :, :] = bias.astype(BF)


def send_kernel(table_ref, asked_ref, out_ref):
    owners, cap = asked_ref.shape
    rows = table_ref.shape[1]
    w2 = table_ref.shape[0] - 16
    table = table_ref[...]
    for o in range(0, owners, 4):
        hot = one_hot(rows, lane_index(asked_ref, o, 4))
        got = mm(table, hot)
        for k in range(4):
            block = got[:, k * cap : (k + 1) * cap]
            out_ref[o + k, 0 : w2 // 2, :] = fold(block[:w2]).astype(BF)
            out_ref[o + k, w2 // 2 :, :] = widen(block[w2 : w2 + 8]).astype(BF)


def hot_kernel(asked_ref, out_ref):
    for o in range(0, asked_ref.shape[0], 4):
        index = lane_index(asked_ref, o, 4)
        n = index.shape[1]
        out_ref[:, o // 4 * n : (o // 4 + 1) * n] = one_hot(out_ref.shape[0], index)


def user_kernel(user_ref, uid_ref, out_ref):
    users = user_ref.shape[0]
    table = jnp.transpose(user_ref[...].astype(F32)).astype(BF)
    step = uid_ref.shape[1]
    for r in range(0, uid_ref.shape[0], 2):
        hot = one_hot(users, lane_index(uid_ref, r, 2))
        out_ref[:, r * step : (r + 2) * step] = mm(table, hot).astype(BF)


def flatten(in_ref, flat, cap):
    owners, width = in_ref.shape[0], in_ref.shape[1] - 8
    for o in range(0, owners, 2):
        cols = slice(o * cap, (o + 2) * cap)
        flat[0:width, cols] = pair(in_ref, o, slice(0, width), 0, cap).astype(BF)
        flat[width : 2 * width, cols] = pair(in_ref, o, slice(0, width), 1, cap).astype(BF)
        bias = pair(in_ref, o, slice(width, width + 8), 0, cap)
        bias = jnp.concatenate([bias, jnp.zeros(bias.shape, F32)], axis=0)
        flat[2 * width :, cols] = bias.astype(BF)


def triple_kernel(
    got_ref, user_ref, uid_ref, pos_ref, neg_ref, send_ref, ugrad_ref, flat, diff, grad, ugd
):
    owners, cap = got_ref.shape[0], got_ref.shape[2] // 2
    width = got_ref.shape[1] - 8
    w2 = 2 * width
    high = w2 + 16
    slots = owners * cap
    triples = user_ref.shape[1]
    users = ugrad_ref.shape[0]
    flatten(got_ref, flat, cap)
    step = 2 * pos_ref.shape[1]
    table = flat[...]
    for r in range(0, pos_ref.shape[0], 2):
        cols = slice(r // 2 * step, (r // 2 + 1) * step)
        diff[:, cols] = signed_hot(slots, lane_index(pos_ref, r, 2), lane_index(neg_ref, r, 2))
        delta = mm(table, diff[:, cols])
        u = user_ref[:, cols].astype(F32)
        x = jnp.sum(u * delta[:w2], axis=0, keepdims=True) + delta[w2 : w2 + 1]
        g = -jax.nn.sigmoid(-x)
        hi, lo = split(g * u)
        first = lax.broadcasted_iota(jnp.int32, (16, step), 0) == 0
        bhi, blo = split(jnp.where(first, g, 0.0))
        grad[0:w2, cols] = hi
        grad[w2:high, cols] = bhi
        grad[high : high + w2, cols] = lo
        grad[high + w2 :, cols] = blo
        hi, lo = split(g * delta[:w2])
        ugd[0:w2, cols] = hi
        ugd[w2:, cols] = lo
    both = grad[...]
    for o in range(0, owners, 4):
        out = mm(both, diff[o * cap : (o + 4) * cap, :], NT)
        out = out[:high] + out[high:]
        for k in range(4):
            block = out[:, k * cap : (k + 1) * cap]
            send_ref[o + k, 0:width, :] = fold(block[:w2]).astype(BF)
            send_ref[o + k, width:, :] = widen(block[w2 : w2 + 8]).astype(BF)
    hot = one_hot(users, lane_index(uid_ref, 0, uid_ref.shape[0]))
    both = mm(hot, ugd[...], NT)
    ugrad_ref[...] = both[:, :w2] + both[:, w2:]


def term_kernel(back_ref, hot_ref, feat_ref, out_ref, flat):
    owners, cap = back_ref.shape[0], back_ref.shape[2] // 2
    width = back_ref.shape[1] - 8
    for o in range(0, owners, 2):
        cols = slice(o * cap, (o + 2) * cap)
        flat[:, cols] = pair(back_ref, o, slice(0, width), 1, cap).astype(BF)
    hi, lo = split(mm(flat[...], hot_ref[...], NT))
    both = mm(jnp.concatenate([hi, lo], axis=0), feat_ref[...])
    term = both[:width] + both[width:]
    across = term.shape[1] // 128
    tiles = width // 8 * across
    per = out_ref.shape[1] // 8
    for t in range(owners * per):
        o, k = divmod(t, per)
        i, j = divmod(t, across)
        tile = jnp.zeros((8, 128), F32)
        if t < tiles:
            tile = term[8 * i : 8 * i + 8, 128 * j : 128 * j + 128]
        out_ref[o, 8 * k : 8 * k + 8, :] = tile


def row_kernel(back_ref, hot_ref, lat_ref, bias_ref, flat):
    owners, cap = back_ref.shape[0], back_ref.shape[2] // 2
    width = lat_ref.shape[0]
    for o in range(0, owners, 2):
        cols = slice(o * cap, (o + 2) * cap)
        flat[0:width, cols] = pair(back_ref, o, slice(0, width), 0, cap).astype(BF)
        bias = pair(back_ref, o, slice(width, width + 8), 0, cap)
        flat[width:, cols] = jnp.concatenate([bias, jnp.zeros(bias.shape, F32)], axis=0).astype(BF)
    total = mm(flat[...], hot_ref[...], NT)
    lat_ref[...] = total[:width]
    bias_ref[...] = total[width : width + 1]


def sum_kernel(in_ref, out_ref, *, scale):
    total = in_ref[0].astype(F32)
    for k in range(1, in_ref.shape[0]):
        total = total + in_ref[k].astype(F32)
    out_ref[...] = jnp.broadcast_to((total * scale)[None], out_ref.shape).astype(out_ref.dtype)


def join_kernel(in_ref, out_ref):
    across = out_ref.shape[1] // 128
    per = in_ref.shape[1] // 8
    for o in range(out_ref.shape[0] // 8 * across // per):
        block = in_ref[o].astype(F32)
        for k in range(per):
            i, j = divmod(o * per + k, across)
            out_ref[8 * i : 8 * i + 8, 128 * j : 128 * j + 128] = block[8 * k : 8 * k + 8]


def call(kernel, out, *args, scratch=(), limit=8, flops=0, moved=0, **more):
    many = isinstance(out, (list, tuple))
    more.setdefault("in_specs", [VM] * len(args))
    more.setdefault("out_specs", [VM] * len(out) if many else VM)
    return pl.pallas_call(
        kernel,
        out_shape=out,
        scratch_shapes=list(scratch),
        compiler_params=pltpu.CompilerParams(vmem_limit_bytes=limit * MIB),
        cost_estimate=pl.CostEstimate(flops=flops, bytes_accessed=moved, transcendentals=0),
        **more,
    )(*args)


def shape(dims, dtype):
    return jax.ShapeDtypeStruct(dims, dtype)


def exchange(x, axis):
    return lax.all_to_all(x, axis, split_axis=0, concat_axis=0, tiled=True)


def on_device(
    item_feat,
    item_latent,
    item_bias,
    projection,
    user_factors,
    user_ids,
    requests,
    pos_slot,
    neg_slot,
):
    owners = lax.axis_size("item")
    groups = lax.axis_size("batch")
    rows, feats = item_feat.shape
    width = item_latent.shape[1]
    users = user_factors.shape[0]
    cap = requests.shape[-1]
    slots = owners * cap
    triples = pos_slot.shape[0]
    w2 = 2 * width
    high = w2 + 16
    lines = triples // 128

    asked = exchange(requests.reshape(owners, cap), "item")
    table = call(
        table_kernel,
        shape((high, rows), BF),
        item_feat,
        item_latent.T,
        item_bias.reshape(1, rows),
        projection.T,
        flops=2 * rows * feats * width,
        moved=2 * rows * (feats + high),
    )
    pos = pos_slot.reshape(lines, 128)
    neg = neg_slot.reshape(lines, 128)
    uid = user_ids.reshape(lines, 128)
    user_rows = call(
        user_kernel,
        shape((w2, triples), BF),
        user_factors,
        uid,
        flops=2 * users * w2 * triples,
        moved=4 * w2 * triples,
    )
    message = shape((owners, width + 8, 2 * cap), BF)
    sent = call(send_kernel, message, table, asked, flops=2 * rows * slots * high)
    got = exchange(sent, "item")
    back, user_grad = call(
        triple_kernel,
        [message, shape((users, w2), F32)],
        got,
        user_rows,
        uid,
        pos,
        neg,
        scratch=[
            pltpu.VMEM((high, slots), BF),
            pltpu.VMEM((slots, triples), BF),
            pltpu.VMEM((2 * high, triples), BF),
            pltpu.VMEM((2 * w2, triples), BF),
        ],
        limit=24,
        flops=6 * slots * triples * high,
    )
    hot = call(
        hot_kernel,
        shape((rows, slots), BF),
        asked,
        flops=4 * slots * rows,
        moved=2 * slots * rows,
    )
    back = exchange(back, "item")
    tiles = width // 8 * (feats // 128)
    chunk = -(-tiles // owners) * 8
    term = call(
        term_kernel,
        shape((owners, chunk, 128), F32),
        back,
        hot,
        item_feat,
        scratch=[pltpu.VMEM((width, slots), BF)],
        flops=2 * rows * slots * high,
    )
    parts = exchange(term, "item")
    lat_grad, bias_grad = call(
        row_kernel,
        [shape((width, rows), F32), shape((1, rows), F32)],
        back,
        hot,
        scratch=[pltpu.VMEM((width + 16, slots), BF)],
        flops=2 * rows * slots * high,
    )
    total = triples * groups * owners
    group_sum = call(
        functools.partial(sum_kernel, scale=1.0), shape((groups, chunk, 128), BF), parts
    )
    parts = exchange(group_sum, "batch")
    whole = call(
        functools.partial(sum_kernel, scale=1.0 / math.sqrt(total)),
        shape((owners, chunk, 128), BF),
        parts,
    )
    parts = exchange(whole, "item")
    projection_grad = call(join_kernel, shape((width, feats), F32), parts)
    return (lat_grad.T, bias_grad.reshape(rows), user_grad, projection_grad.T)


def solution(mesh):
    placed = (
        P(("batch", "item"), None),
        P(("batch", "item"), None),
        P(("batch", "item")),
        P(),
        P(("batch", "item"), None),
        P(("batch", "item")),
        P("batch", "item", None, None),
        P(("batch", "item")),
        P(("batch", "item")),
    )
    return jax.shard_map(
        on_device,
        mesh=mesh,
        in_specs=placed,
        out_specs=(
            P(("batch", "item"), None),
            P(("batch", "item")),
            P(("batch", "item"), None),
            P(),
        ),
        check_vma=False,
    )
```

time: 116 us -> 111 us (0.957)
  blocking collectives: 68.4 us -> 36.9 us
  waiting for transfers between devices: 15.7 us -> 33.2 us
  starting transfers between devices: 14.7 us -> 24.3 us
    all_to_all x4 -> x2, blocking collectives: 68.4 us -> 36.9 us  [exchange(): return lax.all_to_all(x, axis, split_axis=0, concat_axis=0, tiled=True)]
    all_to_all x2 -> x4, waiting for transfers between devices: 15.7 us -> 33.2 us  [exchange(): return lax.all_to_all(x, axis, split_axis=0, concat_axis=0, tiled=True)]
    all_to_all x2 -> x4, starting transfers between devices: 14.7 us -> 24.3 us  [exchange(): return lax.all_to_all(x, axis, split_axis=0, concat_axis=0, tiled=True)]
    pallas_call x8 -> x10, Pallas kernels: 13 us -> 11.9 us  [call(): pl.pallas_call(kernel, out_shape=out, scratch_shapes=list(scratch), compi...]
    unnamed x18 -> x16, local copies, waits for them, and re-layouts: 2.89 us -> 2.88 us
  transfers between devices with their start and end apart: 2 -> 4, of which waited for: 2 -> 4; matrix products, arithmetic and copies ran while one was open for 0% -> 1% of each run, Pallas kernels for 1% -> 2%
where the time goes in v2:
time: 111 us
  blocking collectives  36.9 us (33%)
  waiting for transfers between devices  33.2 us (30%)
  starting transfers between devices  24.3 us (22%)
  Pallas kernels  11.9 us (11%)
  local copies, waits for them, and re-layouts  3.57 us (3%)
    all_to_all x2, blocking collectives, exchange(): return lax.all_to_all(x, axis, split_axis=0, concat_axis=0, tiled=True)  36.9 us
    all_to_all x4, waiting for transfers between devices, exchange(): return lax.all_to_all(x, axis, split_axis=0, concat_axis=0, tiled=True)  33.2 us
    all_to_all x4, starting transfers between devices, exchange(): return lax.all_to_all(x, axis, split_axis=0, concat_axis=0, tiled=True)  24.3 us
    pallas_call x10, Pallas kernels, call(): pl.pallas_call(kernel, out_shape=out, scratch_shapes=list(scratch), compi...  11.9 us
    unnamed x16, local copies, waits for them, and re-layouts  2.88 us
  transfers between devices with their start and end apart: 4, of which 4 were waited for; matrix products, arithmetic and copies ran while one was open for 1% of the time, Pallas kernels for 2%

profile of v2, /device:TPU:1, one launch (start us, length us, event | category | flops | bytes accessed | tf_op | source)
XLA Modules:
  0.0 110.6 jit_solution(8783166800831276478)
XLA Ops:
  0.6 0.0 copy-start.5
  0.7 10.5 %all-to-all-start = ((s32[32,1,64]{2,1,0:T(1,128)}), s32[32,1,64]{2,1,0:T(1,128)S(1)}, u32[]{:S(2)}, u32[]{:S(2)}) async-start(s32[32,1,64]{2,1,0:T(1,128)} %bitcast.19), calls=%async_computation | async-start | bytes 32768 | tf_op jit(solution)/shard_map/all_to_all | solution.py:232
  11.2 0.7 reshape.27.bias_ref
  11.9 1.1 %copy-done = bf16[512,768]{1,0:T(8,128)(2,1)S(1)} copy-done((bf16[512,768]{1,0:T(8,128)(2,1)S(1)}, bf16[512,768]{1,0:T(8,128)(2,1)}, u32[]{:S(2)}) %copy-start) | copy-done | bytes 786456
  13.0 0.9 copy-done.2
  13.9 0.8 copy-done.3
  14.7 0.4 shard_map.120.table_ref
  15.1 3.1 %all-to-all-done = s32[32,1,64]{2,1,0:T(1,128)S(1)} async-done(((s32[32,1,64]{2,1,0:T(1,128)}), s32[32,1,64]{2,1,0:T(1,128)S(1)}, u32[]{:S(2)}, u32[]{:S(2)}) %all-to-all-start) | async-done | bytes 8224 | tf_op jit(solution)/shard_map/all_to_all | solution.py:232
  18.2 1.5 %shard_map.121 = bf16[32,72,128]{2,1,0:T(8,128)(2,1)} custom-call(bf16[144,512]{1,0:T(8,128)(2,1)S(1)} %shard_map.120.table_ref, s32[32,64]{1,0:T(8,128)S(1)} %bitcast.11), custom_call_target="tpu_custom_call" | custom-call | flops 301989888 | tf_op jit(solution)/shard_map/pallas_call | solution.py:217
  19.6 4.4 %all-to-all-start.1 = ((bf16[32,72,128]{2,1,0:T(8,128)(2,1)}), bf16[32,72,128]{2,1,0:T(8,128)(2,1)S(1)}, u32[]{:S(2)}, u32[]{:S(2)}) async-start(bf16[32,72,128]{2,1,0:T(8,128)(2,1)} %shard_map.121), calls=%async_computation.1 | async-start | bytes 1179648 | tf_op jit(solution)/shard_map/all_to_all | solution.py:232
  24.1 0.3 shard_map.122.user_ref
  24.4 11.9 %all-to-all-done.1.got_ref = bf16[32,72,128]{2,1,0:T(8,128)(2,1)S(1)} async-done(((bf16[32,72,128]{2,1,0:T(8,128)(2,1)}), bf16[32,72,128]{2,1,0:T(8,128)(2,1)S(1)}, u32[]{:S(2)}, u32[]{:S(2)}) %all-to-all-start.1) | async-done | bytes 589856 | tf_op jit(solution)/shard_map/all_to_all | solution.py:232
  36.3 5.5 %shard_map.123 = (bf16[32,72,128]{2,1,0:T(8,128)(2,1)}, f32[256,128]{1,0:T(8,128)}) custom-call(bf16[32,72,128]{2,1,0:T(8,128)(2,1)S(1)} %all-to-all-done.1.got_ref, bf16[128,2048]{1,0:T(8,128)(2,1)S(1)} %shard_map.122.user_ref, s32[16,128]{1,0:T(8,128)S(1)} %bitcast.15, s32[16,128]{1,0:T(8,128)S(1)} %bitcast.16, s32[16,128]{1,0:T(8,128)S(1)} %bitcast.17), custom_call_target="tpu_custom_call" | custom-call | flops 3623878656 | tf_op jit(solution)/shard_map/pallas_call | solution.py:217
  41.8 3.8 %all-to-all-start.2 = ((bf16[32,72,128]{2,1,0:T(8,128)(2,1)}), bf16[32,72,128]{2,1,0:T(8,128)(2,1)S(1)}, u32[]{:S(2)}, u32[]{:S(2)}) async-start(bf16[32,72,128]{2,1,0:T(8,128)(2,1)} %get-tuple-element.8), calls=%async_computation.2 | async-start | bytes 1179648 | tf_op jit(solution)/shard_map/all_to_all | solution.py:232
  45.7 0.4 shard_map.124.hot_ref
  46.1 11.9 %all-to-all-done.2.back_ref = bf16[32,72,128]{2,1,0:T(8,128)(2,1)S(1)} async-done(((bf16[32,72,128]{2,1,0:T(8,128)(2,1)}), bf16[32,72,128]{2,1,0:T(8,128)(2,1)S(1)}, u32[]{:S(2)}, u32[]{:S(2)}) %all-to-all-start.2) | async-done | bytes 589856 | tf_op jit(solution)/shard_map/all_to_all | solution.py:232
  57.9 1.0 shard_map.126
  59.0 12.5 %all_to_all.36.in_ref = f32[32,16,128]{2,1,0:T(8,128)S(1)} all-to-all(f32[32,16,128]{2,1,0:T(8,128)S(1)} %shard_map.126), channel_id=1, replica_groups=mesh['batch'=16,'item'=32] {'item'}, dimensions={0} | all-to-all | bytes 524288 | tf_op jit(solution)/shard_map/all_to_all | solution.py:232
  71.5 24.4 %all_to_all.37.in_ref = bf16[16,16,128]{2,1,0:T(8,128)(2,1)S(1)} all-to-all(bf16[16,16,128]{2,1,0:T(8,128)(2,1)S(1)} %shard_map.127), channel_id=1, replica_groups=mesh['batch'=16,'item'=32] {'batch'}, dimensions={0} | all-to-all | bytes 131072 | tf_op jit(solution)/shard_map/all_to_all | solution.py:232
  95.9 0.7 shard_map.128
  96.6 5.5 %all-to-all-start.5 = ((bf16[32,16,128]{2,1,0:T(8,128)(2,1)}), bf16[32,16,128]{2,1,0:T(8,128)(2,1)S(1)}, u32[]{:S(2)}, u32[]{:S(2)}) async-start(bf16[32,16,128]{2,1,0:T(8,128)(2,1)} %shard_map.128), calls=%async_computation.5 | async-start | bytes 262144 | tf_op jit(solution)/shard_map/all_to_all | solution.py:232
  102.1 1.4 %shard_map.125 = (f32[64,512]{1,0:T(8,128)}, f32[1,512]{1,0:T(1,128)}) custom-call(bf16[32,72,128]{2,1,0:T(8,128)(2,1)S(1)} %all-to-all-done.2.back_ref, bf16[512,2048]{1,0:T(8,128)(2,1)S(1)} %shard_map.124.hot_ref), custom_call_target="tpu_custom_call" | custom-call | flops 301989888 | tf_op jit(solution)/shard_map/pallas_call | solution.py:217
  103.5 6.4 %all-to-all-done.5.in_ref = bf16[32,16,128]{2,1,0:T(8,128)(2,1)S(1)} async-done(((bf16[32,16,128]{2,1,0:T(8,128)(2,1)}), bf16[32,16,128]{2,1,0:T(8,128)(2,1)S(1)}, u32[]{:S(2)}, u32[]{:S(2)}) %all-to-all-start.5) | async-done | bytes 131104 | tf_op jit(solution)/shard_map/all_to_all | solution.py:232
  109.9 0.7 shard_map.129
  (13 shorter events, 0.1 us)
Async XLA Ops:
  0.6 23.4 %copy-start.5 = (s32[2048]{0:T(1024)S(1)}, s32[2048]{0:T(1024)}, u32[]{:S(2)}) copy-start(s32[2048]{0:T(1024)} %param.14) | copy-start | bytes 24580
  0.6 35.7 %copy-start.6 = (s32[2048]{0:T(1024)S(1)}, s32[2048]{0:T(1024)}, u32[]{:S(2)}) copy-start(s32[2048]{0:T(1024)} %param.16) | copy-start | bytes 24580
  0.7 35.7 %copy-start.7 = (s32[2048]{0:T(1024)S(1)}, s32[2048]{0:T(1024)}, u32[]{:S(2)}) copy-start(s32[2048]{0:T(1024)} %param.17) | copy-start | bytes 24580
  0.7 17.5 %all-to-all-start = ((s32[32,1,64]{2,1,0:T(1,128)}), s32[32,1,64]{2,1,0:T(1,128)S(1)}, u32[]{:S(2)}, u32[]{:S(2)}) async-start(s32[32,1,64]{2,1,0:T(1,128)} %bitcast.19), calls=%async_computation | async-start | bytes 32768 | tf_op jit(solution)/shard_map/all_to_all | solution.py:232
  11.9 1.1 %copy-start = (bf16[512,768]{1,0:T(8,128)(2,1)S(1)}, bf16[512,768]{1,0:T(8,128)(2,1)}, u32[]{:S(2)}) copy-start(bf16[512,768]{1,0:T(8,128)(2,1)} %feat_ref.3) | copy-start | bytes 2359300
  13.0 0.9 copy-start.2
  13.9 0.8 copy-start.3
  14.7 9.3 %copy-start.4 = (bf16[256,128]{1,0:T(8,128)(2,1)S(1)}, bf16[256,128]{1,0:T(8,128)(2,1)}, u32[]{:S(2)}) copy-start(bf16[256,128]{1,0:T(8,128)(2,1)} %user_ref.1) | copy-start | bytes 196612
  19.6 16.7 %all-to-all-start.1 = ((bf16[32,72,128]{2,1,0:T(8,128)(2,1)}), bf16[32,72,128]{2,1,0:T(8,128)(2,1)S(1)}, u32[]{:S(2)}, u32[]{:S(2)}) async-start(bf16[32,72,128]{2,1,0:T(8,128)(2,1)} %shard_map.121), calls=%async_computation.1 | async-start | bytes 1179648 | tf_op jit(solution)/shard_map/all_to_all | solution.py:232
  41.8 16.1 %copy-start.1 = (bf16[512,768]{1,0:T(8,128)(2,1)S(1)}, bf16[512,768]{1,0:T(8,128)(2,1)}, u32[]{:S(2)}) copy-start(bf16[512,768]{1,0:T(8,128)(2,1)} %feat_ref.3) | copy-start | bytes 2359300
  41.8 16.1 %all-to-all-start.2 = ((bf16[32,72,128]{2,1,0:T(8,128)(2,1)}), bf16[32,72,128]{2,1,0:T(8,128)(2,1)S(1)}, u32[]{:S(2)}, u32[]{:S(2)}) async-start(bf16[32,72,128]{2,1,0:T(8,128)(2,1)} %get-tuple-element.8), calls=%async_computation.2 | async-start | bytes 1179648 | tf_op jit(solution)/shard_map/all_to_all | solution.py:232
  96.6 13.3 %all-to-all-start.5 = ((bf16[32,16,128]{2,1,0:T(8,128)(2,1)}), bf16[32,16,128]{2,1,0:T(8,128)(2,1)S(1)}, u32[]{:S(2)}, u32[]{:S(2)}) async-start(bf16[32,16,128]{2,1,0:T(8,128)(2,1)} %shard_map.128), calls=%async_computation.5 | async-start | bytes 262144 | tf_op jit(solution)/shard_map/all_to_all | solution.py:232

commit v3 on v2

--- a/solution.py
+++ b/solution.py
@@ -89,20 +89,11 @@
             out_ref[o + k, w2 // 2 :, :] = widen(block[w2 : w2 + 8]).astype(BF)
 
 
-def hot_kernel(asked_ref, out_ref):
+def fill_hot(asked_ref, hot):
     for o in range(0, asked_ref.shape[0], 4):
         index = lane_index(asked_ref, o, 4)
         n = index.shape[1]
-        out_ref[:, o // 4 * n : (o // 4 + 1) * n] = one_hot(out_ref.shape[0], index)
-
-
-def user_kernel(user_ref, uid_ref, out_ref):
-    users = user_ref.shape[0]
-    table = jnp.transpose(user_ref[...].astype(F32)).astype(BF)
-    step = uid_ref.shape[1]
-    for r in range(0, uid_ref.shape[0], 2):
-        hot = one_hot(users, lane_index(uid_ref, r, 2))
-        out_ref[:, r * step : (r + 2) * step] = mm(table, hot).astype(BF)
+        hot[:, o // 4 * n : (o // 4 + 1) * n] = one_hot(hot.shape[0], index)
 
 
 def flatten(in_ref, flat, cap):
@@ -117,23 +108,25 @@
 
 
 def triple_kernel(
-    got_ref, user_ref, uid_ref, pos_ref, neg_ref, send_ref, ugrad_ref, flat, diff, grad, ugd
+    got_ref, user_ref, uid_ref, pos_ref, neg_ref, send_ref, ugrad_ref, flat, diff, grad, ugd, picked
 ):
     owners, cap = got_ref.shape[0], got_ref.shape[2] // 2
     width = got_ref.shape[1] - 8
     w2 = 2 * width
     high = w2 + 16
     slots = owners * cap
-    triples = user_ref.shape[1]
-    users = ugrad_ref.shape[0]
+    users = user_ref.shape[0]
     flatten(got_ref, flat, cap)
+    user_table = jnp.transpose(user_ref[...].astype(F32)).astype(BF)
     step = 2 * pos_ref.shape[1]
     table = flat[...]
     for r in range(0, pos_ref.shape[0], 2):
         cols = slice(r // 2 * step, (r // 2 + 1) * step)
         diff[:, cols] = signed_hot(slots, lane_index(pos_ref, r, 2), lane_index(neg_ref, r, 2))
         delta = mm(table, diff[:, cols])
-        u = user_ref[:, cols].astype(F32)
+        mine = one_hot(users, lane_index(uid_ref, r, 2))
+        picked[:, cols] = mine
+        u = mm(user_table, mine)
         x = jnp.sum(u * delta[:w2], axis=0, keepdims=True) + delta[w2 : w2 + 1]
         g = -jax.nn.sigmoid(-x)
         hi, lo = split(g * u)
@@ -154,33 +147,32 @@
             block = out[:, k * cap : (k + 1) * cap]
             send_ref[o + k, 0:width, :] = fold(block[:w2]).astype(BF)
             send_ref[o + k, width:, :] = widen(block[w2 : w2 + 8]).astype(BF)
-    hot = one_hot(users, lane_index(uid_ref, 0, uid_ref.shape[0]))
-    both = mm(hot, ugd[...], NT)
+    both = mm(picked[...], ugd[...], NT)
     ugrad_ref[...] = both[:, :w2] + both[:, w2:]
 
 
-def term_kernel(back_ref, hot_ref, feat_ref, out_ref, flat):
+def block_of(ref, o, chunks):
+    _, lines, span = chunks.shape
+    i, j = divmod(o, ref.shape[1] // span)
+    return ref[i * lines : (i + 1) * lines, j * span : (j + 1) * span]
+
+
+def term_kernel(back_ref, asked_ref, feat_ref, out_ref, flat, hot):
+    fill_hot(asked_ref, hot)
     owners, cap = back_ref.shape[0], back_ref.shape[2] // 2
     width = back_ref.shape[1] - 8
     for o in range(0, owners, 2):
         cols = slice(o * cap, (o + 2) * cap)
         flat[:, cols] = pair(back_ref, o, slice(0, width), 1, cap).astype(BF)
-    hi, lo = split(mm(flat[...], hot_ref[...], NT))
+    hi, lo = split(mm(flat[...], hot[...], NT))
     both = mm(jnp.concatenate([hi, lo], axis=0), feat_ref[...])
     term = both[:width] + both[width:]
-    across = term.shape[1] // 128
-    tiles = width // 8 * across
-    per = out_ref.shape[1] // 8
-    for t in range(owners * per):
-        o, k = divmod(t, per)
-        i, j = divmod(t, across)
-        tile = jnp.zeros((8, 128), F32)
-        if t < tiles:
-            tile = term[8 * i : 8 * i + 8, 128 * j : 128 * j + 128]
-        out_ref[o, 8 * k : 8 * k + 8, :] = tile
-
-
-def row_kernel(back_ref, hot_ref, lat_ref, bias_ref, flat):
+    for o in range(owners):
+        out_ref[o] = block_of(term, o, out_ref)
+
+
+def row_kernel(back_ref, asked_ref, lat_ref, bias_ref, flat, hot):
+    fill_hot(asked_ref, hot)
     owners, cap = back_ref.shape[0], back_ref.shape[2] // 2
     width = lat_ref.shape[0]
     for o in range(0, owners, 2):
@@ -188,7 +180,7 @@
         flat[0:width, cols] = pair(back_ref, o, slice(0, width), 0, cap).astype(BF)
         bias = pair(back_ref, o, slice(width, width + 8), 0, cap)
         flat[width:, cols] = jnp.concatenate([bias, jnp.zeros(bias.shape, F32)], axis=0).astype(BF)
-    total = mm(flat[...], hot_ref[...], NT)
+    total = mm(flat[...], hot[...], NT)
     lat_ref[...] = total[:width]
     bias_ref[...] = total[width : width + 1]
 
@@ -201,13 +193,16 @@
 
 
 def join_kernel(in_ref, out_ref):
-    across = out_ref.shape[1] // 128
-    per = in_ref.shape[1] // 8
-    for o in range(out_ref.shape[0] // 8 * across // per):
-        block = in_ref[o].astype(F32)
-        for k in range(per):
-            i, j = divmod(o * per + k, across)
-            out_ref[8 * i : 8 * i + 8, 128 * j : 128 * j + 128] = block[8 * k : 8 * k + 8]
+    owners, lines, span = in_ref.shape
+    across = out_ref.shape[1] // span
+    for o in range(0, owners, 2 * across):
+        pairs = [
+            jnp.concatenate([in_ref[o + j].astype(F32), in_ref[o + across + j].astype(F32)], axis=0)
+            for j in range(across)
+        ]
+        i = o // across * lines
+        for j in range(across):
+            out_ref[i : i + 2 * lines, j * span : (j + 1) * span] = pairs[j]
 
 
 def call(kernel, out, *args, scratch=(), limit=8, flops=0, moved=0, **more):
@@ -256,6 +251,9 @@
     lines = triples // 128
 
     asked = exchange(requests.reshape(owners, cap), "item")
+    pos = pos_slot.reshape(lines, 128)
+    neg = neg_slot.reshape(lines, 128)
+    uid = user_ids.reshape(lines, 128)
     table = call(
         table_kernel,
         shape((high, rows), BF),
@@ -266,17 +264,6 @@
         flops=2 * rows * feats * width,
         moved=2 * rows * (feats + high),
     )
-    pos = pos_slot.reshape(lines, 128)
-    neg = neg_slot.reshape(lines, 128)
-    uid = user_ids.reshape(lines, 128)
-    user_rows = call(
-        user_kernel,
-        shape((w2, triples), BF),
-        user_factors,
-        uid,
-        flops=2 * users * w2 * triples,
-        moved=4 * w2 * triples,
-    )
     message = shape((owners, width + 8, 2 * cap), BF)
     sent = call(send_kernel, message, table, asked, flops=2 * rows * slots * high)
     got = exchange(sent, "item")
@@ -284,7 +271,7 @@
         triple_kernel,
         [message, shape((users, w2), F32)],
         got,
-        user_rows,
+        user_factors,
         uid,
         pos,
         neg,
@@ -293,27 +280,21 @@
             pltpu.VMEM((slots, triples), BF),
             pltpu.VMEM((2 * high, triples), BF),
             pltpu.VMEM((2 * w2, triples), BF),
+            pltpu.VMEM((users, triples), BF),
         ],
         limit=24,
         flops=6 * slots * triples * high,
     )
-    hot = call(
-        hot_kernel,
-        shape((rows, slots), BF),
-        asked,
-        flops=4 * slots * rows,
-        moved=2 * slots * rows,
-    )
     back = exchange(back, "item")
-    tiles = width // 8 * (feats // 128)
-    chunk = -(-tiles // owners) * 8
+    lines = 4
+    chunk = (lines, width * feats // owners // lines)
     term = call(
         term_kernel,
-        shape((owners, chunk, 128), F32),
+        shape((owners, *chunk), F32),
         back,
-        hot,
+        asked,
         item_feat,
-        scratch=[pltpu.VMEM((width, slots), BF)],
+        scratch=[pltpu.VMEM((width, slots), BF), pltpu.VMEM((rows, slots), BF)],
         flops=2 * rows * slots * high,
     )
     parts = exchange(term, "item")
@@ -321,18 +302,18 @@
         row_kernel,
         [shape((width, rows), F32), shape((1, rows), F32)],
         back,
-        hot,
-        scratch=[pltpu.VMEM((width + 16, slots), BF)],
+        asked,
+        scratch=[pltpu.VMEM((width + 16, slots), BF), pltpu.VMEM((rows, slots), BF)],
         flops=2 * rows * slots * high,
     )
     total = triples * groups * owners
     group_sum = call(
-        functools.partial(sum_kernel, scale=1.0), shape((groups, chunk, 128), BF), parts
+        functools.partial(sum_kernel, scale=1.0), shape((groups, *chunk), BF), parts
     )
     parts = exchange(group_sum, "batch")
     whole = call(
         functools.partial(sum_kernel, scale=1.0 / math.sqrt(total)),
-        shape((owners, chunk, 128), BF),
+        shape((owners, *chunk), BF),
         parts,
     )
     parts = exchange(whole, "item")

time: 111 us -> 108 us (0.973)
  blocking collectives: 36.9 us -> 68.2 us
  waiting for transfers between devices: 33.2 us -> 9.8 us
  starting transfers between devices: 24.3 us -> 15.6 us
  Pallas kernels: 11.9 us -> 10.3 us
    all_to_all x2 -> x4, blocking collectives: 36.9 us -> 68.2 us  [exchange(): return lax.all_to_all(x, axis, split_axis=0, concat_axis=0, tiled=True)]
    all_to_all x4 -> x2, waiting for transfers between devices: 33.2 us -> 9.8 us  [exchange(): return lax.all_to_all(x, axis, split_axis=0, concat_axis=0, tiled=True)]
    all_to_all x4 -> x2, starting transfers between devices: 24.3 us -> 15.6 us  [exchange(): return lax.all_to_all(x, axis, split_axis=0, concat_axis=0, tiled=True)]
    pallas_call x10 -> x8, Pallas kernels: 11.9 us -> 10.3 us  [call(): pl.pallas_call(kernel, out_shape=out, scratch_shapes=list(scratch), compi...]
    unnamed x16 -> x18, local copies, waits for them, and re-layouts: 2.88 us -> 2.89 us
  transfers between devices with their start and end apart: 4 -> 2, of which waited for: 4 -> 2; matrix products, arithmetic and copies ran while one was open for 1% -> 0% of each run, Pallas kernels for 2% -> 2%
where the time goes in v3:
time: 108 us
  blocking collectives  68.2 us (63%)
  starting transfers between devices  15.6 us (14%)
  Pallas kernels  10.3 us (10%)
  waiting for transfers between devices  9.8 us (9%)
  local copies, waits for them, and re-layouts  2.9 us (3%)
    all_to_all x4, blocking collectives, exchange(): return lax.all_to_all(x, axis, split_axis=0, concat_axis=0, tiled=True)  68.2 us
    all_to_all x2, starting transfers between devices, exchange(): return lax.all_to_all(x, axis, split_axis=0, concat_axis=0, tiled=True)  15.6 us
    pallas_call x8, Pallas kernels, call(): pl.pallas_call(kernel, out_shape=out, scratch_shapes=list(scratch), compi...  10.3 us
    all_to_all x2, waiting for transfers between devices, exchange(): return lax.all_to_all(x, axis, split_axis=0, concat_axis=0, tiled=True)  9.8 us
    unnamed x18, local copies, waits for them, and re-layouts  2.89 us
  transfers between devices with their start and end apart: 2, of which 2 were waited for; matrix products, arithmetic and copies ran while one was open for 0% of the time, Pallas kernels for 2%

profile of v3, /device:TPU:1, one launch (start us, length us, event | category | flops | bytes accessed | tf_op | source)
XLA Modules:
  0.0 107.6 jit_solution(18361268867161390323)
XLA Ops:
  0.6 10.4 %all-to-all-start = ((s32[32,1,64]{2,1,0:T(1,128)}), s32[32,1,64]{2,1,0:T(1,128)S(1)}, u32[]{:S(2)}, u32[]{:S(2)}) async-start(s32[32,1,64]{2,1,0:T(1,128)} %bitcast.19), calls=%async_computation | async-start | bytes 32768 | tf_op jit(solution)/shard_map/all_to_all | solution.py:227
  11.0 0.0 copy-done.8
  11.0 0.0 copy-start
  11.1 1.1 %copy-done = bf16[512,768]{1,0:T(8,128)(2,1)S(1)} copy-done((bf16[512,768]{1,0:T(8,128)(2,1)S(1)}, bf16[512,768]{1,0:T(8,128)(2,1)}, u32[]{:S(2)}) %copy-start) | copy-done | bytes 786456
  12.2 0.9 copy-done.2
  13.1 0.8 copy-done.3
  13.9 0.4 shard_map.120.table_ref
  14.3 3.7 %all-to-all-done = s32[32,1,64]{2,1,0:T(1,128)S(1)} async-done(((s32[32,1,64]{2,1,0:T(1,128)}), s32[32,1,64]{2,1,0:T(1,128)S(1)}, u32[]{:S(2)}, u32[]{:S(2)}) %all-to-all-start) | async-done | bytes 8224 | tf_op jit(solution)/shard_map/all_to_all | solution.py:227
  18.0 0.6 shard_map.121
  18.6 0.0 copy-start.4
  18.7 0.0 copy-start.5
  18.7 0.0 copy-start.6
  18.7 0.0 copy-start.7
  18.7 16.1 %all_to_all.36.got_ref = bf16[32,72,128]{2,1,0:T(8,128)(2,1)S(1)} all-to-all(bf16[32,72,128]{2,1,0:T(8,128)(2,1)S(1)} %shard_map.121), channel_id=1, replica_groups=mesh['batch'=16,'item'=32] {'item'}, dimensions={0} | all-to-all | bytes 1179648 | tf_op jit(solution)/shard_map/all_to_all | solution.py:227
  34.8 5.4 %shard_map.122 = (bf16[32,72,128]{2,1,0:T(8,128)(2,1)S(1)}, f32[256,128]{1,0:T(8,128)}) custom-call(bf16[32,72,128]{2,1,0:T(8,128)(2,1)S(1)} %all_to_all.36.got_ref, bf16[256,128]{1,0:T(8,128)(2,1)S(1)} %copy-done.4, s32[16,128]{1,0:T(8,128)S(1)} %bitcast.15, s32[16,128]{1,0:T(8,128)S(1)} %bitcast.16, s32[16,128]{1,0:T(8,128)S(1)} %bitcast.17), custom_call_target="tpu_custom_call" | custom-call | flops 3623878656 | tf_op jit(solution)/shard_map/pallas_call | solution.py:212
  40.2 15.9 %all_to_all.37.back_ref = bf16[32,72,128]{2,1,0:T(8,128)(2,1)S(1)} all-to-all(bf16[32,72,128]{2,1,0:T(8,128)(2,1)S(1)} %get-tuple-element.8), channel_id=1, replica_groups=mesh['batch'=16,'item'=32] {'item'}, dimensions={0} | all-to-all | bytes 1179648 | tf_op jit(solution)/shard_map/all_to_all | solution.py:227
  56.1 1.1 shard_map.124
  57.2 11.8 %all_to_all.38.in_ref = f32[32,4,384]{2,1,0:T(4,128)S(1)} all-to-all(f32[32,4,384]{2,1,0:T(4,128)S(1)} %shard_map.124), channel_id=1, replica_groups=mesh['batch'=16,'item'=32] {'item'}, dimensions={0} | all-to-all | bytes 393216 | tf_op jit(solution)/shard_map/all_to_all | solution.py:227
  69.0 24.4 %all_to_all.39.in_ref = bf16[16,4,384]{2,1,0:T(4,128)(2,1)S(1)} all-to-all(bf16[16,4,384]{2,1,0:T(4,128)(2,1)S(1)} %shard_map.125), channel_id=1, replica_groups=mesh['batch'=16,'item'=32] {'batch'}, dimensions={0} | all-to-all | bytes 98304 | tf_op jit(solution)/shard_map/all_to_all | solution.py:227
  93.4 0.7 shard_map.126
  94.1 5.2 %all-to-all-start.5 = ((bf16[32,4,384]{2,1,0:T(4,128)(2,1)}), bf16[32,4,384]{2,1,0:T(4,128)(2,1)S(1)}, u32[]{:S(2)}, u32[]{:S(2)}) async-start(bf16[32,4,384]{2,1,0:T(4,128)(2,1)} %shard_map.126), calls=%async_computation.5 | async-start | bytes 196608 | tf_op jit(solution)/shard_map/all_to_all | solution.py:227
  99.3 1.5 %shard_map.123 = (f32[64,512]{1,0:T(8,128)}, f32[1,512]{1,0:T(1,128)}) custom-call(bf16[32,72,128]{2,1,0:T(8,128)(2,1)S(1)} %all_to_all.37.back_ref, s32[32,64]{1,0:T(8,128)S(1)} %bitcast.13), custom_call_target="tpu_custom_call" | custom-call | flops 301989888 | tf_op jit(solution)/shard_map/pallas_call | solution.py:212
  100.8 6.1 %all-to-all-done.5.in_ref = bf16[32,4,384]{2,1,0:T(4,128)(2,1)S(1)} async-done(((bf16[32,4,384]{2,1,0:T(4,128)(2,1)}), bf16[32,4,384]{2,1,0:T(4,128)(2,1)S(1)}, u32[]{:S(2)}, u32[]{:S(2)}) %all-to-all-start.5) | async-done | bytes 98336 | tf_op jit(solution)/shard_map/all_to_all | solution.py:227
  106.9 0.7 shard_map.127
  (11 shorter events, 0.1 us)
Async XLA Ops:
  0.6 10.4 %copy-start.8 = (bf16[512]{0:T(512)(128)(2,1)S(1)}, bf16[512]{0:T(512)(128)(2,1)}, u32[]{:S(2)}) copy-start(bf16[512]{0:T(512)(128)(2,1)} %param.11) | copy-start | bytes 3076
  0.6 17.4 %all-to-all-start = ((s32[32,1,64]{2,1,0:T(1,128)}), s32[32,1,64]{2,1,0:T(1,128)S(1)}, u32[]{:S(2)}, u32[]{:S(2)}) async-start(s32[32,1,64]{2,1,0:T(1,128)} %bitcast.19), calls=%async_computation | async-start | bytes 32768 | tf_op jit(solution)/shard_map/all_to_all | solution.py:227
  11.0 1.1 %copy-start = (bf16[512,768]{1,0:T(8,128)(2,1)S(1)}, bf16[512,768]{1,0:T(8,128)(2,1)}, u32[]{:S(2)}) copy-start(bf16[512,768]{1,0:T(8,128)(2,1)} %feat_ref.3) | copy-start | bytes 2359300
  12.2 0.9 copy-start.2
  13.1 0.8 copy-start.3
  18.6 16.2 %copy-start.4 = (bf16[256,128]{1,0:T(8,128)(2,1)S(1)}, bf16[256,128]{1,0:T(8,128)(2,1)}, u32[]{:S(2)}) copy-start(bf16[256,128]{1,0:T(8,128)(2,1)} %user_ref.1) | copy-start | bytes 196612
  18.7 16.2 %copy-start.5 = (s32[2048]{0:T(1024)S(1)}, s32[2048]{0:T(1024)}, u32[]{:S(2)}) copy-start(s32[2048]{0:T(1024)} %param.14) | copy-start | bytes 24580
  18.7 16.2 %copy-start.6 = (s32[2048]{0:T(1024)S(1)}, s32[2048]{0:T(1024)}, u32[]{:S(2)}) copy-start(s32[2048]{0:T(1024)} %param.16) | copy-start | bytes 24580
  18.7 16.1 %copy-start.7 = (s32[2048]{0:T(1024)S(1)}, s32[2048]{0:T(1024)}, u32[]{:S(2)}) copy-start(s32[2048]{0:T(1024)} %param.17) | copy-start | bytes 24580
  40.2 15.9 %copy-start.1 = (bf16[512,768]{1,0:T(8,128)(2,1)S(1)}, bf16[512,768]{1,0:T(8,128)(2,1)}, u32[]{:S(2)}) copy-start(bf16[512,768]{1,0:T(8,128)(2,1)} %feat_ref.3) | copy-start | bytes 2359300
  94.1 12.8 %all-to-all-start.5 = ((bf16[32,4,384]{2,1,0:T(4,128)(2,1)}), bf16[32,4,384]{2,1,0:T(4,128)(2,1)S(1)}, u32[]{:S(2)}, u32[]{:S(2)}) async-start(bf16[32,4,384]{2,1,0:T(4,128)(2,1)} %shard_map.126), calls=%async_computation.5 | async-start | bytes 196608 | tf_op jit(solution)/shard_map/all_to_all | solution.py:227

commit v4 on v3

--- a/solution.py
+++ b/solution.py
@@ -11,6 +11,7 @@
 BF = jnp.bfloat16
 F32 = jnp.float32
 VM = pl.BlockSpec(memory_space=pltpu.VMEM)
+ANY = pl.BlockSpec(memory_space=pl.ANY)
 NN = (((1,), (0,)), ((), ()))
 NT = (((1,), (1,)), ((), ()))
 MIB = 1024 * 1024
@@ -89,13 +90,6 @@
             out_ref[o + k, w2 // 2 :, :] = widen(block[w2 : w2 + 8]).astype(BF)
 
 
-def fill_hot(asked_ref, hot):
-    for o in range(0, asked_ref.shape[0], 4):
-        index = lane_index(asked_ref, o, 4)
-        n = index.shape[1]
-        hot[:, o // 4 * n : (o // 4 + 1) * n] = one_hot(hot.shape[0], index)
-
-
 def flatten(in_ref, flat, cap):
     owners, width = in_ref.shape[0], in_ref.shape[1] - 8
     for o in range(0, owners, 2):
@@ -108,7 +102,7 @@
 
 
 def triple_kernel(
-    got_ref, user_ref, uid_ref, pos_ref, neg_ref, send_ref, ugrad_ref, flat, diff, grad, ugd, picked
+    got_ref, user_ref, uid_ref, pos_ref, neg_ref, send_ref, ugrad_out, flat, diff, grad, ugd, picked, ugrad, sem
 ):
     owners, cap = got_ref.shape[0], got_ref.shape[2] // 2
     width = got_ref.shape[1] - 8
@@ -139,6 +133,10 @@
         hi, lo = split(g * delta[:w2])
         ugd[0:w2, cols] = hi
         ugd[w2:, cols] = lo
+    both = mm(picked[...], ugd[...], NT)
+    ugrad[...] = both[:, :w2] + both[:, w2:]
+    copy = pltpu.make_async_copy(ugrad, ugrad_out, sem)
+    copy.start()
     both = grad[...]
     for o in range(0, owners, 4):
         out = mm(both, diff[o * cap : (o + 4) * cap, :], NT)
@@ -147,8 +145,7 @@
             block = out[:, k * cap : (k + 1) * cap]
             send_ref[o + k, 0:width, :] = fold(block[:w2]).astype(BF)
             send_ref[o + k, width:, :] = widen(block[w2 : w2 + 8]).astype(BF)
-    both = mm(picked[...], ugd[...], NT)
-    ugrad_ref[...] = both[:, :w2] + both[:, w2:]
+    copy.wait()
 
 
 def block_of(ref, o, chunks):
@@ -157,32 +154,37 @@
     return ref[i * lines : (i + 1) * lines, j * span : (j + 1) * span]
 
 
-def term_kernel(back_ref, asked_ref, feat_ref, out_ref, flat, hot):
-    fill_hot(asked_ref, hot)
-    owners, cap = back_ref.shape[0], back_ref.shape[2] // 2
+def term_kernel(
+    back_ref, asked_ref, feat_ref, lat_out, bias_out, out_ref, lat_ref, bias_ref, sems
+):
+    owners, cap = asked_ref.shape
     width = back_ref.shape[1] - 8
-    for o in range(0, owners, 2):
-        cols = slice(o * cap, (o + 2) * cap)
-        flat[:, cols] = pair(back_ref, o, slice(0, width), 1, cap).astype(BF)
-    hi, lo = split(mm(flat[...], hot[...], NT))
+    rows = feat_ref.shape[0]
+    total = jnp.zeros((2 * width + 16, rows), F32)
+    for o in range(0, owners, 8):
+        parts = []
+        for k in range(o, o + 8, 2):
+            bias = pair(back_ref, k, slice(width, width + 8), 0, cap)
+            both = [pair(back_ref, k, slice(0, width), side, cap) for side in range(2)]
+            parts.append(jnp.concatenate([*both, bias, jnp.zeros(bias.shape, F32)], axis=0))
+        part = jnp.concatenate(parts, axis=1).astype(BF)
+        total = total + mm(part, one_hot(rows, lane_index(asked_ref, o, 8)), NT)
+    lat_ref[...] = total[:width]
+    bias_ref[...] = total[2 * width : 2 * width + 1]
+    copies = [
+        pltpu.make_async_copy(lat_ref, lat_out, sems.at[0]),
+        pltpu.make_async_copy(bias_ref, bias_out, sems.at[1]),
+    ]
+    for copy in copies:
+        copy.start()
+    total = total[width : 2 * width]
+    hi, lo = split(total)
     both = mm(jnp.concatenate([hi, lo], axis=0), feat_ref[...])
     term = both[:width] + both[width:]
     for o in range(owners):
         out_ref[o] = block_of(term, o, out_ref)
-
-
-def row_kernel(back_ref, asked_ref, lat_ref, bias_ref, flat, hot):
-    fill_hot(asked_ref, hot)
-    owners, cap = back_ref.shape[0], back_ref.shape[2] // 2
-    width = lat_ref.shape[0]
-    for o in range(0, owners, 2):
-        cols = slice(o * cap, (o + 2) * cap)
-        flat[0:width, cols] = pair(back_ref, o, slice(0, width), 0, cap).astype(BF)
-        bias = pair(back_ref, o, slice(width, width + 8), 0, cap)
-        flat[width:, cols] = jnp.concatenate([bias, jnp.zeros(bias.shape, F32)], axis=0).astype(BF)
-    total = mm(flat[...], hot[...], NT)
-    lat_ref[...] = total[:width]
-    bias_ref[...] = total[width : width + 1]
+    for copy in copies:
+        copy.wait()
 
 
 def sum_kernel(in_ref, out_ref, *, scale):
@@ -281,31 +283,31 @@
             pltpu.VMEM((2 * high, triples), BF),
             pltpu.VMEM((2 * w2, triples), BF),
             pltpu.VMEM((users, triples), BF),
+            pltpu.VMEM((users, w2), F32),
+            pltpu.SemaphoreType.DMA,
         ],
+        out_specs=[VM, ANY],
         limit=24,
         flops=6 * slots * triples * high,
     )
     back = exchange(back, "item")
     lines = 4
     chunk = (lines, width * feats // owners // lines)
-    term = call(
+    lat_grad, bias_grad, term = call(
         term_kernel,
-        shape((owners, *chunk), F32),
+        [shape((width, rows), F32), shape((1, rows), F32), shape((owners, *chunk), F32)],
         back,
         asked,
         item_feat,
-        scratch=[pltpu.VMEM((width, slots), BF), pltpu.VMEM((rows, slots), BF)],
+        out_specs=[ANY, ANY, VM],
+        scratch=[
+            pltpu.VMEM((width, rows), F32),
+            pltpu.VMEM((1, rows), F32),
+            pltpu.SemaphoreType.DMA((2,)),
+        ],
         flops=2 * rows * slots * high,
     )
     parts = exchange(term, "item")
-    lat_grad, bias_grad = call(
-        row_kernel,
-        [shape((width, rows), F32), shape((1, rows), F32)],
-        back,
-        asked,
-        scratch=[pltpu.VMEM((width + 16, slots), BF), pltpu.VMEM((rows, slots), BF)],
-        flops=2 * rows * slots * high,
-    )
     total = triples * groups * owners
     group_sum = call(
         functools.partial(sum_kernel, scale=1.0), shape((groups, *chunk), BF), parts

time: 108 us -> 107 us (level)
  blocking collectives: 68.2 us -> 80.6 us
  waiting for transfers between devices: 9.8 us -> 3.73 us
  starting transfers between devices: 15.6 us -> 10.4 us
  Pallas kernels: 10.3 us -> 8.09 us
    all_to_all x4 -> x5, blocking collectives: 68.2 us -> 80.6 us  [exchange(): return lax.all_to_all(x, axis, split_axis=0, concat_axis=0, tiled=True)]
    all_to_all x2 -> x1, waiting for transfers between devices: 9.8 us -> 3.73 us  [exchange(): return lax.all_to_all(x, axis, split_axis=0, concat_axis=0, tiled=True)]
    all_to_all x2 -> x1, starting transfers between devices: 15.6 us -> 10.4 us  [exchange(): return lax.all_to_all(x, axis, split_axis=0, concat_axis=0, tiled=True)]
    pallas_call x8 -> x7, Pallas kernels: 10.3 us -> 8.09 us  [call(): pl.pallas_call(kernel, out_shape=out, scratch_shapes=list(scratch), compi...]
  transfers between devices with their start and end apart: 2 -> 1, of which waited for: 2 -> 1; matrix products, arithmetic and copies ran while one was open for 0% -> 0% of each run, Pallas kernels for 2% -> 0%
where the time goes in v4:
time: 107 us; the launch traced here: 106 us
  blocking collectives  80.6 us (75%)
  starting transfers between devices  10.4 us (10%)
  Pallas kernels  8.09 us (8%)
  waiting for transfers between devices  3.73 us (3%)
  local copies, waits for them, and re-layouts  2.9 us (3%)
    all_to_all x5, blocking collectives, exchange(): return lax.all_to_all(x, axis, split_axis=0, concat_axis=0, tiled=True)  80.6 us
    all_to_all x1, starting transfers between devices, exchange(): return lax.all_to_all(x, axis, split_axis=0, concat_axis=0, tiled=True)  10.4 us
    pallas_call x7, Pallas kernels, call(): pl.pallas_call(kernel, out_shape=out, scratch_shapes=list(scratch), compi...  8.09 us
    all_to_all x1, waiting for transfers between devices, exchange(): return lax.all_to_all(x, axis, split_axis=0, concat_axis=0, tiled=True)  3.73 us
    unnamed x18, local copies, waits for them, and re-layouts  2.9 us
  transfers between devices with their start and end apart: 1, of which 1 were waited for; matrix products, arithmetic and copies ran while one was open for 0% of the time, Pallas kernels for 0%

profile of v4, /device:TPU:1, one launch (start us, length us, event | category | flops | bytes accessed | tf_op | source)
XLA Modules:
  0.0 106.4 jit_solution(10701445751975166742)
XLA Ops:
  0.6 10.4 %all-to-all-start = ((s32[32,1,64]{2,1,0:T(1,128)}), s32[32,1,64]{2,1,0:T(1,128)S(1)}, u32[]{:S(2)}, u32[]{:S(2)}) async-start(s32[32,1,64]{2,1,0:T(1,128)} %bitcast.18), calls=%async_computation | async-start | bytes 32768 | tf_op jit(solution)/shard_map/all_to_all | solution.py:229
  11.0 0.0 copy-done.8
  11.0 0.0 copy-start
  11.1 1.1 %copy-done = bf16[512,768]{1,0:T(8,128)(2,1)S(1)} copy-done((bf16[512,768]{1,0:T(8,128)(2,1)S(1)}, bf16[512,768]{1,0:T(8,128)(2,1)}, u32[]{:S(2)}) %copy-start) | copy-done | bytes 786456
  12.2 0.9 copy-done.2
  13.1 0.8 copy-done.3
  13.9 0.4 shard_map.120.table_ref
  14.3 3.7 %all-to-all-done = s32[32,1,64]{2,1,0:T(1,128)S(1)} async-done(((s32[32,1,64]{2,1,0:T(1,128)}), s32[32,1,64]{2,1,0:T(1,128)S(1)}, u32[]{:S(2)}, u32[]{:S(2)}) %all-to-all-start) | async-done | bytes 8224 | tf_op jit(solution)/shard_map/all_to_all | solution.py:229
  18.0 0.6 shard_map.121
  18.6 0.0 copy-start.4
  18.7 0.0 copy-start.5
  18.7 0.0 copy-start.6
  18.7 0.0 copy-start.7
  18.7 16.1 %all_to_all.36.got_ref = bf16[32,72,128]{2,1,0:T(8,128)(2,1)S(1)} all-to-all(bf16[32,72,128]{2,1,0:T(8,128)(2,1)S(1)} %shard_map.121), channel_id=1, replica_groups=mesh['batch'=16,'item'=32] {'item'}, dimensions={0} | all-to-all | bytes 1179648 | tf_op jit(solution)/shard_map/all_to_all | solution.py:229
  34.8 0.0 copy-done.4
  34.8 0.0 copy-done.6
  34.8 4.8 %shard_map.122 = (bf16[32,72,128]{2,1,0:T(8,128)(2,1)S(1)}, f32[256,128]{1,0:T(8,128)}) custom-call(bf16[32,72,128]{2,1,0:T(8,128)(2,1)S(1)} %all_to_all.36.got_ref, bf16[256,128]{1,0:T(8,128)(2,1)S(1)} %copy-done.4, s32[16,128]{1,0:T(8,128)S(1)} %bitcast.14, s32[16,128]{1,0:T(8,128)S(1)} %bitcast.15, s32[16,128]{1,0:T(8,128)S(1)} %bitcast.16), custom_call_target="tpu_custom_call" | custom-call | flops 3623878656 | tf_op jit(solution)/shard_map/pallas_call | solution.py:214
  39.6 0.0 copy-start.1
  39.6 15.9 %all_to_all.37.back_ref = bf16[32,72,128]{2,1,0:T(8,128)(2,1)S(1)} all-to-all(bf16[32,72,128]{2,1,0:T(8,128)(2,1)S(1)} %get-tuple-element.9), channel_id=1, replica_groups=mesh['batch'=16,'item'=32] {'item'}, dimensions={0} | all-to-all | bytes 1179648 | tf_op jit(solution)/shard_map/all_to_all | solution.py:229
  55.5 1.6 %shard_map.123 = (f32[64,512]{1,0:T(8,128)}, f32[1,512]{1,0:T(1,128)}, f32[32,4,384]{2,1,0:T(4,128)S(1)}) custom-call(bf16[32,72,128]{2,1,0:T(8,128)(2,1)S(1)} %all_to_all.37.back_ref, s32[32,64]{1,0:T(8,128)S(1)} %bitcast.12, bf16[512,768]{1,0:T(8,128)(2,1)S(1)} %copy-done.1), custom_call_target="tpu_custom_call" | custom-call | flops 301989888 | tf_op jit(solution)/shard_map/pallas_call | solution.py:214
  57.1 11.8 %all_to_all.38.in_ref = f32[32,4,384]{2,1,0:T(4,128)S(1)} all-to-all(f32[32,4,384]{2,1,0:T(4,128)S(1)} %get-tuple-element.13), channel_id=1, replica_groups=mesh['batch'=16,'item'=32] {'item'}, dimensions={0} | all-to-all | bytes 393216 | tf_op jit(solution)/shard_map/all_to_all | solution.py:229
  68.9 24.4 %all_to_all.39.in_ref = bf16[16,4,384]{2,1,0:T(4,128)(2,1)S(1)} all-to-all(bf16[16,4,384]{2,1,0:T(4,128)(2,1)S(1)} %shard_map.124), channel_id=1, replica_groups=mesh['batch'=16,'item'=32] {'batch'}, dimensions={0} | all-to-all | bytes 98304 | tf_op jit(solution)/shard_map/all_to_all | solution.py:229
  93.4 12.4 %all_to_all.40.in_ref = bf16[32,4,384]{2,1,0:T(4,128)(2,1)S(1)} all-to-all(bf16[32,4,384]{2,1,0:T(4,128)(2,1)S(1)} %shard_map.125), channel_id=1, replica_groups=mesh['batch'=16,'item'=32] {'item'}, dimensions={0} | all-to-all | bytes 196608 | tf_op jit(solution)/shard_map/all_to_all | solution.py:229
  105.7 0.7 shard_map.126
  (9 shorter events, 0.1 us)
Async XLA Ops:
  0.6 10.4 %copy-start.8 = (bf16[512]{0:T(512)(128)(2,1)S(1)}, bf16[512]{0:T(512)(128)(2,1)}, u32[]{:S(2)}) copy-start(bf16[512]{0:T(512)(128)(2,1)} %param.11) | copy-start | bytes 3076
  0.6 17.4 %all-to-all-start = ((s32[32,1,64]{2,1,0:T(1,128)}), s32[32,1,64]{2,1,0:T(1,128)S(1)}, u32[]{:S(2)}, u32[]{:S(2)}) async-start(s32[32,1,64]{2,1,0:T(1,128)} %bitcast.18), calls=%async_computation | async-start | bytes 32768 | tf_op jit(solution)/shard_map/all_to_all | solution.py:229
  11.0 1.1 %copy-start = (bf16[512,768]{1,0:T(8,128)(2,1)S(1)}, bf16[512,768]{1,0:T(8,128)(2,1)}, u32[]{:S(2)}) copy-start(bf16[512,768]{1,0:T(8,128)(2,1)} %feat_ref.3) | copy-start | bytes 2359300
  12.2 0.9 copy-start.2
  13.1 0.8 copy-start.3
  18.6 16.2 %copy-start.4 = (bf16[256,128]{1,0:T(8,128)(2,1)S(1)}, bf16[256,128]{1,0:T(8,128)(2,1)}, u32[]{:S(2)}) copy-start(bf16[256,128]{1,0:T(8,128)(2,1)} %user_ref.1) | copy-start | bytes 196612
  18.7 16.2 %copy-start.5 = (s32[2048]{0:T(1024)S(1)}, s32[2048]{0:T(1024)}, u32[]{:S(2)}) copy-start(s32[2048]{0:T(1024)} %param.14) | copy-start | bytes 24580
  18.7 16.2 %copy-start.6 = (s32[2048]{0:T(1024)S(1)}, s32[2048]{0:T(1024)}, u32[]{:S(2)}) copy-start(s32[2048]{0:T(1024)} %param.16) | copy-start | bytes 24580
  18.7 16.1 %copy-start.7 = (s32[2048]{0:T(1024)S(1)}, s32[2048]{0:T(1024)}, u32[]{:S(2)}) copy-start(s32[2048]{0:T(1024)} %param.17) | copy-start | bytes 24580
  39.6 15.9 %copy-start.1 = (bf16[512,768]{1,0:T(8,128)(2,1)S(1)}, bf16[512,768]{1,0:T(8,128)(2,1)}, u32[]{:S(2)}) copy-start(bf16[512,768]{1,0:T(8,128)(2,1)} %feat_ref.3) | copy-start | bytes 2359300

commit v5 on v4

--- a/solution.py
+++ b/solution.py
@@ -154,9 +154,7 @@
     return ref[i * lines : (i + 1) * lines, j * span : (j + 1) * span]
 
 
-def term_kernel(
-    back_ref, asked_ref, feat_ref, lat_out, bias_out, out_ref, lat_ref, bias_ref, sems
-):
+def term_kernel(back_ref, asked_ref, feat_ref, lat_ref, bias_ref, out_ref):
     owners, cap = asked_ref.shape
     width = back_ref.shape[1] - 8
     rows = feat_ref.shape[0]
@@ -171,20 +169,12 @@
         total = total + mm(part, one_hot(rows, lane_index(asked_ref, o, 8)), NT)
     lat_ref[...] = total[:width]
     bias_ref[...] = total[2 * width : 2 * width + 1]
-    copies = [
-        pltpu.make_async_copy(lat_ref, lat_out, sems.at[0]),
-        pltpu.make_async_copy(bias_ref, bias_out, sems.at[1]),
-    ]
-    for copy in copies:
-        copy.start()
     total = total[width : 2 * width]
     hi, lo = split(total)
     both = mm(jnp.concatenate([hi, lo], axis=0), feat_ref[...])
     term = both[:width] + both[width:]
     for o in range(owners):
         out_ref[o] = block_of(term, o, out_ref)
-    for copy in copies:
-        copy.wait()
 
 
 def sum_kernel(in_ref, out_ref, *, scale):
@@ -194,17 +184,22 @@
     out_ref[...] = jnp.broadcast_to((total * scale)[None], out_ref.shape).astype(out_ref.dtype)
 
 
-def join_kernel(in_ref, out_ref):
+def join_kernel(in_ref, lat_ref, bias_ref, out_hbm, lat_hbm, bias_hbm, out_ref, sems):
+    moves = [(lat_ref, lat_hbm), (bias_ref, bias_hbm), (out_ref, out_hbm)]
+    copies = [pltpu.make_async_copy(a, b, sems.at[i]) for i, (a, b) in enumerate(moves)]
+    for copy in copies[:2]:
+        copy.start()
     owners, lines, span = in_ref.shape
     across = out_ref.shape[1] // span
     for o in range(0, owners, 2 * across):
-        pairs = [
-            jnp.concatenate([in_ref[o + j].astype(F32), in_ref[o + across + j].astype(F32)], axis=0)
-            for j in range(across)
-        ]
         i = o // across * lines
         for j in range(across):
-            out_ref[i : i + 2 * lines, j * span : (j + 1) * span] = pairs[j]
+            pair = [in_ref[o + j].astype(F32), in_ref[o + across + j].astype(F32)]
+            columns = slice(j * span, (j + 1) * span)
+            out_ref[i : i + 2 * lines, columns] = jnp.concatenate(pair, axis=0)
+    copies[2].start()
+    for copy in copies:
+        copy.wait()
 
 
 def call(kernel, out, *args, scratch=(), limit=8, flops=0, moved=0, **more):
@@ -299,12 +294,6 @@
         back,
         asked,
         item_feat,
-        out_specs=[ANY, ANY, VM],
-        scratch=[
-            pltpu.VMEM((width, rows), F32),
-            pltpu.VMEM((1, rows), F32),
-            pltpu.SemaphoreType.DMA((2,)),
-        ],
         flops=2 * rows * slots * high,
     )
     parts = exchange(term, "item")
@@ -319,7 +308,15 @@
         parts,
     )
     parts = exchange(whole, "item")
-    projection_grad = call(join_kernel, shape((width, feats), F32), parts)
+    projection_grad, lat_grad, bias_grad = call(
+        join_kernel,
+        [shape((width, feats), F32), shape((width, rows), F32), shape((1, rows), F32)],
+        parts,
+        lat_grad,
+        bias_grad,
+        out_specs=[ANY] * 3,
+        scratch=[pltpu.VMEM((width, feats), F32), pltpu.SemaphoreType.DMA((3,))],
+    )
     return (lat_grad.T, bias_grad.reshape(rows), user_grad, projection_grad.T)
 
 

time: 107 us -> 107 us (level)
  no operation moved by 1% of the time
where the time goes in v5:
time: 107 us; the launch traced here: 106 us
  blocking collectives  80.6 us (75%)
  starting transfers between devices  10.4 us (10%)
  Pallas kernels  7.72 us (7%)
  waiting for transfers between devices  3.73 us (3%)
  local copies, waits for them, and re-layouts  2.9 us (3%)
    all_to_all x5, blocking collectives, exchange(): return lax.all_to_all(x, axis, split_axis=0, concat_axis=0, tiled=True)  80.6 us
    all_to_all x1, starting transfers between devices, exchange(): return lax.all_to_all(x, axis, split_axis=0, concat_axis=0, tiled=True)  10.4 us
    pallas_call x7, Pallas kernels, call(): pl.pallas_call(kernel, out_shape=out, scratch_shapes=list(scratch), compi...  7.72 us
    all_to_all x1, waiting for transfers between devices, exchange(): return lax.all_to_all(x, axis, split_axis=0, concat_axis=0, tiled=True)  3.73 us
    unnamed x18, local copies, waits for them, and re-layouts  2.9 us
  transfers between devices with their start and end apart: 1, of which 1 were waited for; matrix products, arithmetic and copies ran while one was open for 0% of the time, Pallas kernels for 0%

profile of v5, /device:TPU:1, one launch (start us, length us, event | category | flops | bytes accessed | tf_op | source)
XLA Modules:
  0.0 106.1 jit_solution(16361862549251336587)
XLA Ops:
  0.6 10.4 %all-to-all-start = ((s32[32,1,64]{2,1,0:T(1,128)}), s32[32,1,64]{2,1,0:T(1,128)S(1)}, u32[]{:S(2)}, u32[]{:S(2)}) async-start(s32[32,1,64]{2,1,0:T(1,128)} %bitcast.17), calls=%async_computation | async-start | bytes 32768 | tf_op jit(solution)/shard_map/all_to_all | solution.py:224
  11.0 0.0 copy-done.8
  11.0 0.0 copy-start
  11.1 1.1 %copy-done = bf16[512,768]{1,0:T(8,128)(2,1)S(1)} copy-done((bf16[512,768]{1,0:T(8,128)(2,1)S(1)}, bf16[512,768]{1,0:T(8,128)(2,1)}, u32[]{:S(2)}) %copy-start) | copy-done | bytes 786456
  12.2 0.9 copy-done.2
  13.1 0.8 copy-done.3
  13.9 0.4 shard_map.120.table_ref
  14.3 3.7 %all-to-all-done = s32[32,1,64]{2,1,0:T(1,128)S(1)} async-done(((s32[32,1,64]{2,1,0:T(1,128)}), s32[32,1,64]{2,1,0:T(1,128)S(1)}, u32[]{:S(2)}, u32[]{:S(2)}) %all-to-all-start) | async-done | bytes 8224 | tf_op jit(solution)/shard_map/all_to_all | solution.py:224
  18.0 0.6 shard_map.121
  18.6 0.0 copy-start.4
  18.7 0.0 copy-start.5
  18.7 0.0 copy-start.6
  18.7 0.0 copy-start.7
  18.7 16.1 %all_to_all.36.got_ref = bf16[32,72,128]{2,1,0:T(8,128)(2,1)S(1)} all-to-all(bf16[32,72,128]{2,1,0:T(8,128)(2,1)S(1)} %shard_map.121), channel_id=1, replica_groups=mesh['batch'=16,'item'=32] {'item'}, dimensions={0} | all-to-all | bytes 1179648 | tf_op jit(solution)/shard_map/all_to_all | solution.py:224
  34.8 0.0 copy-done.4
  34.8 0.0 copy-done.6
  34.8 4.8 %shard_map.122 = (bf16[32,72,128]{2,1,0:T(8,128)(2,1)S(1)}, f32[256,128]{1,0:T(8,128)}) custom-call(bf16[32,72,128]{2,1,0:T(8,128)(2,1)S(1)} %all_to_all.36.got_ref, bf16[256,128]{1,0:T(8,128)(2,1)S(1)} %copy-done.4, s32[16,128]{1,0:T(8,128)S(1)} %bitcast.14, s32[16,128]{1,0:T(8,128)S(1)} %bitcast.15, s32[16,128]{1,0:T(8,128)S(1)} %bitcast.16), custom_call_target="tpu_custom_call" | custom-call | flops 3623878656 | tf_op jit(solution)/shard_map/pallas_call | solution.py:209
  39.6 0.0 copy-start.1
  39.6 15.9 %all_to_all.37.back_ref = bf16[32,72,128]{2,1,0:T(8,128)(2,1)S(1)} all-to-all(bf16[32,72,128]{2,1,0:T(8,128)(2,1)S(1)} %get-tuple-element.12), channel_id=1, replica_groups=mesh['batch'=16,'item'=32] {'item'}, dimensions={0} | all-to-all | bytes 1179648 | tf_op jit(solution)/shard_map/all_to_all | solution.py:224
  55.5 1.1 %shard_map.123 = (f32[64,512]{1,0:T(8,128)S(1)}, f32[1,512]{1,0:T(1,128)S(1)}, f32[32,4,384]{2,1,0:T(4,128)S(1)}) custom-call(bf16[32,72,128]{2,1,0:T(8,128)(2,1)S(1)} %all_to_all.37.back_ref, s32[32,64]{1,0:T(8,128)S(1)} %bitcast.12, bf16[512,768]{1,0:T(8,128)(2,1)S(1)} %copy-done.1), custom_call_target="tpu_custom_call" | custom-call | flops 301989888 | tf_op jit(solution)/shard_map/pallas_call | solution.py:209
  56.6 11.8 %all_to_all.38.in_ref = f32[32,4,384]{2,1,0:T(4,128)S(1)} all-to-all(f32[32,4,384]{2,1,0:T(4,128)S(1)} %get-tuple-element.13), channel_id=1, replica_groups=mesh['batch'=16,'item'=32] {'item'}, dimensions={0} | all-to-all | bytes 393216 | tf_op jit(solution)/shard_map/all_to_all | solution.py:224
  68.5 24.4 %all_to_all.39.in_ref = bf16[16,4,384]{2,1,0:T(4,128)(2,1)S(1)} all-to-all(bf16[16,4,384]{2,1,0:T(4,128)(2,1)S(1)} %shard_map.124), channel_id=1, replica_groups=mesh['batch'=16,'item'=32] {'batch'}, dimensions={0} | all-to-all | bytes 98304 | tf_op jit(solution)/shard_map/all_to_all | solution.py:224
  92.9 12.4 %all_to_all.40.in_ref = bf16[32,4,384]{2,1,0:T(4,128)(2,1)S(1)} all-to-all(bf16[32,4,384]{2,1,0:T(4,128)(2,1)S(1)} %shard_map.125), channel_id=1, replica_groups=mesh['batch'=16,'item'=32] {'item'}, dimensions={0} | all-to-all | bytes 196608 | tf_op jit(solution)/shard_map/all_to_all | solution.py:224
  105.3 0.8 shard_map.126
  (9 shorter events, 0.1 us)
Async XLA Ops:
  0.6 10.4 %copy-start.8 = (bf16[512]{0:T(512)(128)(2,1)S(1)}, bf16[512]{0:T(512)(128)(2,1)}, u32[]{:S(2)}) copy-start(bf16[512]{0:T(512)(128)(2,1)} %param.11) | copy-start | bytes 3076
  0.6 17.4 %all-to-all-start = ((s32[32,1,64]{2,1,0:T(1,128)}), s32[32,1,64]{2,1,0:T(1,128)S(1)}, u32[]{:S(2)}, u32[]{:S(2)}) async-start(s32[32,1,64]{2,1,0:T(1,128)} %bitcast.17), calls=%async_computation | async-start | bytes 32768 | tf_op jit(solution)/shard_map/all_to_all | solution.py:224
  11.0 1.1 %copy-start = (bf16[512,768]{1,0:T(8,128)(2,1)S(1)}, bf16[512,768]{1,0:T(8,128)(2,1)}, u32[]{:S(2)}) copy-start(bf16[512,768]{1,0:T(8,128)(2,1)} %feat_ref.3) | copy-start | bytes 2359300
  12.2 0.9 copy-start.2
  13.1 0.8 copy-start.3
  18.6 16.2 %copy-start.4 = (bf16[256,128]{1,0:T(8,128)(2,1)S(1)}, bf16[256,128]{1,0:T(8,128)(2,1)}, u32[]{:S(2)}) copy-start(bf16[256,128]{1,0:T(8,128)(2,1)} %user_ref.1) | copy-start | bytes 196612
  18.7 16.2 %copy-start.5 = (s32[2048]{0:T(1024)S(1)}, s32[2048]{0:T(1024)}, u32[]{:S(2)}) copy-start(s32[2048]{0:T(1024)} %param.14) | copy-start | bytes 24580
  18.7 16.2 %copy-start.6 = (s32[2048]{0:T(1024)S(1)}, s32[2048]{0:T(1024)}, u32[]{:S(2)}) copy-start(s32[2048]{0:T(1024)} %param.16) | copy-start | bytes 24580
  18.7 16.1 %copy-start.7 = (s32[2048]{0:T(1024)S(1)}, s32[2048]{0:T(1024)}, u32[]{:S(2)}) copy-start(s32[2048]{0:T(1024)} %param.17) | copy-start | bytes 24580
  39.6 15.9 %copy-start.1 = (bf16[512,768]{1,0:T(8,128)(2,1)S(1)}, bf16[512,768]{1,0:T(8,128)(2,1)}, u32[]{:S(2)}) copy-start(bf16[512,768]{1,0:T(8,128)(2,1)} %feat_ref.3) | copy-start | bytes 2359300

commit v6 on v5

--- a/solution.py
+++ b/solution.py
@@ -63,8 +63,25 @@
 
 def pair(ref, o, lines, side, cap):
     cols = slice(side * cap, (side + 1) * cap)
-    a, b = ref[o, lines, :].astype(F32), ref[o + 1, lines, :].astype(F32)
+    a, b = take(ref, o)[lines], take(ref, o + 1)[lines]
     return jnp.concatenate([a[:, cols], b[:, cols]], axis=1)
+
+
+def put(ref, o, block, w2):
+    _, parts, lines, span = ref.shape
+    ref[o, : parts - 1] = fold(block[:w2]).astype(BF).reshape(parts - 1, lines, span)
+    ref[o, parts - 1] = widen(block[w2 : w2 + lines]).astype(BF)
+
+
+def width_of(ref):
+    return (ref.shape[1] - 1) * ref.shape[2]
+
+
+def take(ref, o):
+    _, parts, lines, span = ref.shape
+    full = ref[o, : parts - 1].reshape((parts - 1) * lines, span).astype(F32)
+    bias = ref[o, parts - 1].astype(F32)
+    return jnp.concatenate([full, bias, jnp.zeros(bias.shape, F32)], axis=0)
 
 
 def table_kernel(feat_ref, lat_ref, bias_ref, proj_ref, out_ref):
@@ -86,12 +103,11 @@
         got = mm(table, hot)
         for k in range(4):
             block = got[:, k * cap : (k + 1) * cap]
-            out_ref[o + k, 0 : w2 // 2, :] = fold(block[:w2]).astype(BF)
-            out_ref[o + k, w2 // 2 :, :] = widen(block[w2 : w2 + 8]).astype(BF)
+            put(out_ref, o + k, block, w2)
 
 
 def flatten(in_ref, flat, cap):
-    owners, width = in_ref.shape[0], in_ref.shape[1] - 8
+    owners, width = in_ref.shape[0], width_of(in_ref)
     for o in range(0, owners, 2):
         cols = slice(o * cap, (o + 2) * cap)
         flat[0:width, cols] = pair(in_ref, o, slice(0, width), 0, cap).astype(BF)
@@ -104,8 +120,8 @@
 def triple_kernel(
     got_ref, user_ref, uid_ref, pos_ref, neg_ref, send_ref, ugrad_out, flat, diff, grad, ugd, picked, ugrad, sem
 ):
-    owners, cap = got_ref.shape[0], got_ref.shape[2] // 2
-    width = got_ref.shape[1] - 8
+    owners, cap = got_ref.shape[0], got_ref.shape[3] // 2
+    width = width_of(got_ref)
     w2 = 2 * width
     high = w2 + 16
     slots = owners * cap
@@ -143,8 +159,7 @@
         out = out[:high] + out[high:]
         for k in range(4):
             block = out[:, k * cap : (k + 1) * cap]
-            send_ref[o + k, 0:width, :] = fold(block[:w2]).astype(BF)
-            send_ref[o + k, width:, :] = widen(block[w2 : w2 + 8]).astype(BF)
+            put(send_ref, o + k, block, w2)
     copy.wait()
 
 
@@ -156,7 +171,7 @@
 
 def term_kernel(back_ref, asked_ref, feat_ref, lat_ref, bias_ref, out_ref):
     owners, cap = asked_ref.shape
-    width = back_ref.shape[1] - 8
+    width = width_of(back_ref)
     rows = feat_ref.shape[0]
     total = jnp.zeros((2 * width + 16, rows), F32)
     for o in range(0, owners, 8):
@@ -245,12 +260,12 @@
     triples = pos_slot.shape[0]
     w2 = 2 * width
     high = w2 + 16
-    lines = triples // 128
+    rows128 = triples // 128
 
     asked = exchange(requests.reshape(owners, cap), "item")
-    pos = pos_slot.reshape(lines, 128)
-    neg = neg_slot.reshape(lines, 128)
-    uid = user_ids.reshape(lines, 128)
+    pos = pos_slot.reshape(rows128, 128)
+    neg = neg_slot.reshape(rows128, 128)
+    uid = user_ids.reshape(rows128, 128)
     table = call(
         table_kernel,
         shape((high, rows), BF),
@@ -261,7 +276,8 @@
         flops=2 * rows * feats * width,
         moved=2 * rows * (feats + high),
     )
-    message = shape((owners, width + 8, 2 * cap), BF)
+    lines = 4
+    message = shape((owners, width // lines + 1, lines, 2 * cap), BF)
     sent = call(send_kernel, message, table, asked, flops=2 * rows * slots * high)
     got = exchange(sent, "item")
     back, user_grad = call(
@@ -286,7 +302,6 @@
         flops=6 * slots * triples * high,
     )
     back = exchange(back, "item")
-    lines = 4
     chunk = (lines, width * feats // owners // lines)
     lat_grad, bias_grad, term = call(
         term_kernel,

time: 107 us -> 106 us (level)
  no operation moved by 1% of the time
where the time goes in v6:
time: 106 us
  blocking collectives  79.9 us (75%)
  starting transfers between devices  10.4 us (10%)
  Pallas kernels  7.89 us (7%)
  waiting for transfers between devices  3.73 us (4%)
  local copies, waits for them, and re-layouts  2.9 us (3%)
    all_to_all x5, blocking collectives, exchange(): return lax.all_to_all(x, axis, split_axis=0, concat_axis=0, tiled=True)  79.9 us
    all_to_all x1, starting transfers between devices, exchange(): return lax.all_to_all(x, axis, split_axis=0, concat_axis=0, tiled=True)  10.4 us
    pallas_call x7, Pallas kernels, call(): pl.pallas_call(kernel, out_shape=out, scratch_shapes=list(scratch), compi...  7.89 us
    all_to_all x1, waiting for transfers between devices, exchange(): return lax.all_to_all(x, axis, split_axis=0, concat_axis=0, tiled=True)  3.73 us
    unnamed x18, local copies, waits for them, and re-layouts  2.9 us
  transfers between devices with their start and end apart: 1, of which 1 were waited for; matrix products, arithmetic and copies ran while one was open for 0% of the time, Pallas kernels for 0%

profile of v6, /device:TPU:1, one launch (start us, length us, event | category | flops | bytes accessed | tf_op | source)
XLA Modules:
  0.0 105.5 jit_solution(7782554915391365696)
XLA Ops:
  0.6 10.4 %all-to-all-start = ((s32[32,1,64]{2,1,0:T(1,128)}), s32[32,1,64]{2,1,0:T(1,128)S(1)}, u32[]{:S(2)}, u32[]{:S(2)}) async-start(s32[32,1,64]{2,1,0:T(1,128)} %bitcast.17), calls=%async_computation | async-start | bytes 32768 | tf_op jit(solution)/shard_map/all_to_all | solution.py:239
  11.0 0.0 copy-done.8
  11.0 0.0 copy-start
  11.1 1.1 %copy-done = bf16[512,768]{1,0:T(8,128)(2,1)S(1)} copy-done((bf16[512,768]{1,0:T(8,128)(2,1)S(1)}, bf16[512,768]{1,0:T(8,128)(2,1)}, u32[]{:S(2)}) %copy-start) | copy-done | bytes 786456
  12.2 0.9 copy-done.2
  13.1 0.8 copy-done.3
  13.9 0.4 shard_map.120.table_ref
  14.3 3.7 %all-to-all-done = s32[32,1,64]{2,1,0:T(1,128)S(1)} async-done(((s32[32,1,64]{2,1,0:T(1,128)}), s32[32,1,64]{2,1,0:T(1,128)S(1)}, u32[]{:S(2)}, u32[]{:S(2)}) %all-to-all-start) | async-done | bytes 8224 | tf_op jit(solution)/shard_map/all_to_all | solution.py:239
  18.0 0.7 shard_map.121
  18.7 0.0 copy-start.4
  18.7 0.0 copy-start.5
  18.7 0.0 copy-start.6
  18.7 0.0 copy-start.7
  18.7 15.8 %all_to_all.36.got_ref = bf16[32,17,4,128]{3,2,1,0:T(4,128)(2,1)S(1)} all-to-all(bf16[32,17,4,128]{3,2,1,0:T(4,128)(2,1)S(1)} %shard_map.121), channel_id=1, replica_groups=mesh['batch'=16,'item'=32] {'item'}, dimensions={0} | all-to-all | bytes 1114112 | tf_op jit(solution)/shard_map/all_to_all | solution.py:239
  34.5 0.0 copy-done.5
  34.5 4.9 %shard_map.122 = (bf16[32,17,4,128]{3,2,1,0:T(4,128)(2,1)S(1)}, f32[256,128]{1,0:T(8,128)}) custom-call(bf16[32,17,4,128]{3,2,1,0:T(4,128)(2,1)S(1)} %all_to_all.36.got_ref, bf16[256,128]{1,0:T(8,128)(2,1)S(1)} %copy-done.4, s32[16,128]{1,0:T(8,128)S(1)} %bitcast.14, s32[16,128]{1,0:T(8,128)S(1)} %bitcast.15, s32[16,128]{1,0:T(8,128)S(1)} %bitcast.16), custom_call_target="tpu_custom_call" | custom-call | flops 3623878656 | tf_op jit(solution)/shard_map/pallas_call | solution.py:224
  39.4 0.0 copy-start.1
  39.5 15.5 %all_to_all.37.back_ref = bf16[32,17,4,128]{3,2,1,0:T(4,128)(2,1)S(1)} all-to-all(bf16[32,17,4,128]{3,2,1,0:T(4,128)(2,1)S(1)} %get-tuple-element.12), channel_id=1, replica_groups=mesh['batch'=16,'item'=32] {'item'}, dimensions={0} | all-to-all | bytes 1114112 | tf_op jit(solution)/shard_map/all_to_all | solution.py:239
  55.0 0.0 copy-done.1
  55.0 1.1 %shard_map.123 = (f32[64,512]{1,0:T(8,128)S(1)}, f32[1,512]{1,0:T(1,128)S(1)}, f32[32,4,384]{2,1,0:T(4,128)S(1)}) custom-call(bf16[32,17,4,128]{3,2,1,0:T(4,128)(2,1)S(1)} %all_to_all.37.back_ref, s32[32,64]{1,0:T(8,128)S(1)} %bitcast.12, bf16[512,768]{1,0:T(8,128)(2,1)S(1)} %copy-done.1), custom_call_target="tpu_custom_call" | custom-call | flops 301989888 | tf_op jit(solution)/shard_map/pallas_call | solution.py:224
  56.1 11.8 %all_to_all.38.in_ref = f32[32,4,384]{2,1,0:T(4,128)S(1)} all-to-all(f32[32,4,384]{2,1,0:T(4,128)S(1)} %get-tuple-element.13), channel_id=1, replica_groups=mesh['batch'=16,'item'=32] {'item'}, dimensions={0} | all-to-all | bytes 393216 | tf_op jit(solution)/shard_map/all_to_all | solution.py:239
  68.0 24.4 %all_to_all.39.in_ref = bf16[16,4,384]{2,1,0:T(4,128)(2,1)S(1)} all-to-all(bf16[16,4,384]{2,1,0:T(4,128)(2,1)S(1)} %shard_map.124), channel_id=1, replica_groups=mesh['batch'=16,'item'=32] {'batch'}, dimensions={0} | all-to-all | bytes 98304 | tf_op jit(solution)/shard_map/all_to_all | solution.py:239
  92.4 12.4 %all_to_all.40.in_ref = bf16[32,4,384]{2,1,0:T(4,128)(2,1)S(1)} all-to-all(bf16[32,4,384]{2,1,0:T(4,128)(2,1)S(1)} %shard_map.125), channel_id=1, replica_groups=mesh['batch'=16,'item'=32] {'item'}, dimensions={0} | all-to-all | bytes 196608 | tf_op jit(solution)/shard_map/all_to_all | solution.py:239
  104.8 0.8 shard_map.126
  (9 shorter events, 0.1 us)
Async XLA Ops:
  0.6 10.4 %copy-start.8 = (bf16[512]{0:T(512)(128)(2,1)S(1)}, bf16[512]{0:T(512)(128)(2,1)}, u32[]{:S(2)}) copy-start(bf16[512]{0:T(512)(128)(2,1)} %param.11) | copy-start | bytes 3076
  0.6 17.4 %all-to-all-start = ((s32[32,1,64]{2,1,0:T(1,128)}), s32[32,1,64]{2,1,0:T(1,128)S(1)}, u32[]{:S(2)}, u32[]{:S(2)}) async-start(s32[32,1,64]{2,1,0:T(1,128)} %bitcast.17), calls=%async_computation | async-start | bytes 32768 | tf_op jit(solution)/shard_map/all_to_all | solution.py:239
  11.0 1.1 %copy-start = (bf16[512,768]{1,0:T(8,128)(2,1)S(1)}, bf16[512,768]{1,0:T(8,128)(2,1)}, u32[]{:S(2)}) copy-start(bf16[512,768]{1,0:T(8,128)(2,1)} %feat_ref.3) | copy-start | bytes 2359300
  12.2 0.9 copy-start.2
  13.1 0.8 copy-start.3
  18.7 15.8 %copy-start.4 = (bf16[256,128]{1,0:T(8,128)(2,1)S(1)}, bf16[256,128]{1,0:T(8,128)(2,1)}, u32[]{:S(2)}) copy-start(bf16[256,128]{1,0:T(8,128)(2,1)} %user_ref.1) | copy-start | bytes 196612
  18.7 15.8 %copy-start.5 = (s32[2048]{0:T(1024)S(1)}, s32[2048]{0:T(1024)}, u32[]{:S(2)}) copy-start(s32[2048]{0:T(1024)} %param.14) | copy-start | bytes 24580
  18.7 15.8 %copy-start.6 = (s32[2048]{0:T(1024)S(1)}, s32[2048]{0:T(1024)}, u32[]{:S(2)}) copy-start(s32[2048]{0:T(1024)} %param.16) | copy-start | bytes 24580
  18.7 15.8 %copy-start.7 = (s32[2048]{0:T(1024)S(1)}, s32[2048]{0:T(1024)}, u32[]{:S(2)}) copy-start(s32[2048]{0:T(1024)} %param.17) | copy-start | bytes 24580
  39.4 15.5 %copy-start.1 = (bf16[512,768]{1,0:T(8,128)(2,1)S(1)}, bf16[512,768]{1,0:T(8,128)(2,1)}, u32[]{:S(2)}) copy-start(bf16[512,768]{1,0:T(8,128)(2,1)} %feat_ref.3) | copy-start | bytes 2359300

commit v7 on v6

--- a/solution.py
+++ b/solution.py
@@ -84,10 +84,11 @@
     return jnp.concatenate([full, bias, jnp.zeros(bias.shape, F32)], axis=0)
 
 
-def table_kernel(feat_ref, lat_ref, bias_ref, proj_ref, out_ref):
-    width, rows = lat_ref.shape
-    out_ref[0:width, :] = lat_ref[...]
-    out_ref[width : 2 * width, :] = mm(proj_ref[...], feat_ref[...], NT).astype(BF)
+def table_kernel(feat_ref, both_ref, bias_ref, out_ref):
+    rows, feats = feat_ref.shape
+    width = both_ref.shape[0]
+    out_ref[0:width, :] = both_ref[:, feats:]
+    out_ref[width : 2 * width, :] = mm(both_ref[:, :feats], feat_ref[...], NT).astype(BF)
     first = lax.broadcasted_iota(jnp.int32, (16, rows), 0) == 0
     bias = jnp.where(first, bias_ref[...].astype(F32), 0.0)
     out_ref[2 * width :, :] = bias.astype(BF)
@@ -154,10 +155,10 @@
     copy = pltpu.make_async_copy(ugrad, ugrad_out, sem)
     copy.start()
     both = grad[...]
-    for o in range(0, owners, 4):
-        out = mm(both, diff[o * cap : (o + 4) * cap, :], NT)
+    for o in range(0, owners, 8):
+        out = mm(both, diff[o * cap : (o + 8) * cap, :], NT)
         out = out[:high] + out[high:]
-        for k in range(4):
+        for k in range(8):
             block = out[:, k * cap : (k + 1) * cap]
             put(send_ref, o + k, block, w2)
     copy.wait()
@@ -270,9 +271,8 @@
         table_kernel,
         shape((high, rows), BF),
         item_feat,
-        item_latent.T,
+        jnp.concatenate([projection.T, item_latent.T], axis=1),
         item_bias.reshape(1, rows),
-        projection.T,
         flops=2 * rows * feats * width,
         moved=2 * rows * (feats + high),
     )

time: 106 us -> 106 us (level)
  local copies, waits for them, and re-layouts: 2.9 us -> 1.17 us
    unnamed x18 -> x14, local copies, waits for them, and re-layouts: 2.9 us -> 1.17 us
  transfers between devices with their start and end apart: 1 -> 1, of which waited for: 1 -> 1; matrix products, arithmetic and copies ran while one was open for 0% -> 1% of each run, Pallas kernels for 0% -> 0%
where the time goes in v7:
time: 106 us
  blocking collectives  79.9 us (75%)
  starting transfers between devices  10.4 us (10%)
  Pallas kernels  7.89 us (7%)
  waiting for transfers between devices  4.5 us (4%)
  local copies, waits for them, and re-layouts  1.17 us (1%)
    all_to_all x5, blocking collectives, exchange(): return lax.all_to_all(x, axis, split_axis=0, concat_axis=0, tiled=True)  79.9 us
    all_to_all x1, starting transfers between devices, exchange(): return lax.all_to_all(x, axis, split_axis=0, concat_axis=0, tiled=True)  10.4 us
    pallas_call x7, Pallas kernels, call(): pl.pallas_call(kernel, out_shape=out, scratch_shapes=list(scratch), compi...  7.89 us
    all_to_all x1, waiting for transfers between devices, exchange(): return lax.all_to_all(x, axis, split_axis=0, concat_axis=0, tiled=True)  4.5 us
  transfers between devices with their start and end apart: 1, of which 1 were waited for; matrix products, arithmetic and copies ran while one was open for 1% of the time, Pallas kernels for 0%

profile of v7, /device:TPU:1, one launch (start us, length us, event | category | flops | bytes accessed | tf_op | source)
XLA Modules:
  0.0 105.5 jit_solution(1000016802020168846)
XLA Ops:
  0.6 10.4 %all-to-all-start = ((s32[32,1,64]{2,1,0:T(1,128)}), s32[32,1,64]{2,1,0:T(1,128)S(1)}, u32[]{:S(2)}, u32[]{:S(2)}) async-start(s32[32,1,64]{2,1,0:T(1,128)} %bitcast.17), calls=%async_computation | async-start | bytes 32768 | tf_op jit(solution)/shard_map/all_to_all | solution.py:240
  11.0 0.0 copy-start.6
  11.0 0.9 pad_maximum_fusion.both_ref
  12.0 0.0 copy-done.6
  12.0 0.0 copy-start
  12.0 1.1 %copy-done = bf16[512,768]{1,0:T(8,128)(2,1)S(1)} copy-done((bf16[512,768]{1,0:T(8,128)(2,1)S(1)}, bf16[512,768]{1,0:T(8,128)(2,1)}, u32[]{:S(2)}) %copy-start) | copy-done | bytes 786456
  13.1 0.4 shard_map.120.table_ref
  13.5 4.5 %all-to-all-done = s32[32,1,64]{2,1,0:T(1,128)S(1)} async-done(((s32[32,1,64]{2,1,0:T(1,128)}), s32[32,1,64]{2,1,0:T(1,128)S(1)}, u32[]{:S(2)}, u32[]{:S(2)}) %all-to-all-start) | async-done | bytes 8224 | tf_op jit(solution)/shard_map/all_to_all | solution.py:240
  18.0 0.7 shard_map.121
  18.7 0.0 copy-start.2
  18.7 0.0 copy-start.3
  18.7 0.0 copy-start.4
  18.7 0.0 copy-start.5
  18.7 15.8 %all_to_all.36.got_ref = bf16[32,17,4,128]{3,2,1,0:T(4,128)(2,1)S(1)} all-to-all(bf16[32,17,4,128]{3,2,1,0:T(4,128)(2,1)S(1)} %shard_map.121), channel_id=1, replica_groups=mesh['batch'=16,'item'=32] {'item'}, dimensions={0} | all-to-all | bytes 1114112 | tf_op jit(solution)/shard_map/all_to_all | solution.py:240
  34.5 0.0 copy-done.2
  34.5 0.0 copy-done.4
  34.5 4.9 %shard_map.122 = (bf16[32,17,4,128]{3,2,1,0:T(4,128)(2,1)S(1)}, f32[256,128]{1,0:T(8,128)}) custom-call(bf16[32,17,4,128]{3,2,1,0:T(4,128)(2,1)S(1)} %all_to_all.36.got_ref, bf16[256,128]{1,0:T(8,128)(2,1)S(1)} %copy-done.2, s32[16,128]{1,0:T(8,128)S(1)} %bitcast.12, s32[16,128]{1,0:T(8,128)S(1)} %bitcast.13, s32[16,128]{1,0:T(8,128)S(1)} %bitcast.14), custom_call_target="tpu_custom_call" | custom-call | flops 3623878656 | tf_op jit(solution)/shard_map/pallas_call | solution.py:225
  39.4 0.0 copy-start.1
  39.5 15.5 %all_to_all.37.back_ref = bf16[32,17,4,128]{3,2,1,0:T(4,128)(2,1)S(1)} all-to-all(bf16[32,17,4,128]{3,2,1,0:T(4,128)(2,1)S(1)} %get-tuple-element.12), channel_id=1, replica_groups=mesh['batch'=16,'item'=32] {'item'}, dimensions={0} | all-to-all | bytes 1114112 | tf_op jit(solution)/shard_map/all_to_all | solution.py:240
  55.0 1.1 %shard_map.123 = (f32[64,512]{1,0:T(8,128)S(1)}, f32[1,512]{1,0:T(1,128)S(1)}, f32[32,4,384]{2,1,0:T(4,128)S(1)}) custom-call(bf16[32,17,4,128]{3,2,1,0:T(4,128)(2,1)S(1)} %all_to_all.37.back_ref, s32[32,64]{1,0:T(8,128)S(1)} %bitcast.11, bf16[512,768]{1,0:T(8,128)(2,1)S(1)} %copy-done.1), custom_call_target="tpu_custom_call" | custom-call | flops 301989888 | tf_op jit(solution)/shard_map/pallas_call | solution.py:225
  56.1 11.8 %all_to_all.38.in_ref = f32[32,4,384]{2,1,0:T(4,128)S(1)} all-to-all(f32[32,4,384]{2,1,0:T(4,128)S(1)} %get-tuple-element.13), channel_id=1, replica_groups=mesh['batch'=16,'item'=32] {'item'}, dimensions={0} | all-to-all | bytes 393216 | tf_op jit(solution)/shard_map/all_to_all | solution.py:240
  68.0 24.4 %all_to_all.39.in_ref = bf16[16,4,384]{2,1,0:T(4,128)(2,1)S(1)} all-to-all(bf16[16,4,384]{2,1,0:T(4,128)(2,1)S(1)} %shard_map.124), channel_id=1, replica_groups=mesh['batch'=16,'item'=32] {'batch'}, dimensions={0} | all-to-all | bytes 98304 | tf_op jit(solution)/shard_map/all_to_all | solution.py:240
  92.4 12.4 %all_to_all.40.in_ref = bf16[32,4,384]{2,1,0:T(4,128)(2,1)S(1)} all-to-all(bf16[32,4,384]{2,1,0:T(4,128)(2,1)S(1)} %shard_map.125), channel_id=1, replica_groups=mesh['batch'=16,'item'=32] {'item'}, dimensions={0} | all-to-all | bytes 196608 | tf_op jit(solution)/shard_map/all_to_all | solution.py:240
  104.8 0.8 shard_map.126
  (6 shorter events, 0.1 us)
Async XLA Ops:
  0.6 17.4 %all-to-all-start = ((s32[32,1,64]{2,1,0:T(1,128)}), s32[32,1,64]{2,1,0:T(1,128)S(1)}, u32[]{:S(2)}, u32[]{:S(2)}) async-start(s32[32,1,64]{2,1,0:T(1,128)} %bitcast.17), calls=%async_computation | async-start | bytes 32768 | tf_op jit(solution)/shard_map/all_to_all | solution.py:240
  11.0 1.0 copy-start.6
  12.0 1.1 %copy-start = (bf16[512,768]{1,0:T(8,128)(2,1)S(1)}, bf16[512,768]{1,0:T(8,128)(2,1)}, u32[]{:S(2)}) copy-start(bf16[512,768]{1,0:T(8,128)(2,1)} %feat_ref.3) | copy-start | bytes 2359300
  18.7 15.8 %copy-start.2 = (bf16[256,128]{1,0:T(8,128)(2,1)S(1)}, bf16[256,128]{1,0:T(8,128)(2,1)}, u32[]{:S(2)}) copy-start(bf16[256,128]{1,0:T(8,128)(2,1)} %user_ref.1) | copy-start | bytes 196612
  18.7 15.8 %copy-start.3 = (s32[2048]{0:T(1024)S(1)}, s32[2048]{0:T(1024)}, u32[]{:S(2)}) copy-start(s32[2048]{0:T(1024)} %param.14) | copy-start | bytes 24580
  18.7 15.8 %copy-start.4 = (s32[2048]{0:T(1024)S(1)}, s32[2048]{0:T(1024)}, u32[]{:S(2)}) copy-start(s32[2048]{0:T(1024)} %param.16) | copy-start | bytes 24580
  18.7 15.8 %copy-start.5 = (s32[2048]{0:T(1024)S(1)}, s32[2048]{0:T(1024)}, u32[]{:S(2)}) copy-start(s32[2048]{0:T(1024)} %param.17) | copy-start | bytes 24580
  39.4 15.5 %copy-start.1 = (bf16[512,768]{1,0:T(8,128)(2,1)S(1)}, bf16[512,768]{1,0:T(8,128)(2,1)}, u32[]{:S(2)}) copy-start(bf16[512,768]{1,0:T(8,128)(2,1)} %feat_ref.3) | copy-start | bytes 2359300

commit v8 on v7

--- a/solution.py
+++ b/solution.py
@@ -155,10 +155,10 @@
     copy = pltpu.make_async_copy(ugrad, ugrad_out, sem)
     copy.start()
     both = grad[...]
-    for o in range(0, owners, 8):
-        out = mm(both, diff[o * cap : (o + 8) * cap, :], NT)
+    for o in range(0, owners, 16):
+        out = mm(both, diff[o * cap : (o + 16) * cap, :], NT)
         out = out[:high] + out[high:]
-        for k in range(8):
+        for k in range(16):
             block = out[:, k * cap : (k + 1) * cap]
             put(send_ref, o + k, block, w2)
     copy.wait()

time: 106 us -> 106 us (level)
  no operation moved by 1% of the time
where the time goes in v8:
time: 106 us
  blocking collectives  79.9 us (75%)
  starting transfers between devices  10.4 us (10%)
  Pallas kernels  7.89 us (7%)
  waiting for transfers between devices  4.5 us (4%)
  local copies, waits for them, and re-layouts  1.17 us (1%)
    all_to_all x5, blocking collectives, exchange(): return lax.all_to_all(x, axis, split_axis=0, concat_axis=0, tiled=True)  79.9 us
    all_to_all x1, starting transfers between devices, exchange(): return lax.all_to_all(x, axis, split_axis=0, concat_axis=0, tiled=True)  10.4 us
    pallas_call x7, Pallas kernels, call(): pl.pallas_call(kernel, out_shape=out, scratch_shapes=list(scratch), compi...  7.89 us
    all_to_all x1, waiting for transfers between devices, exchange(): return lax.all_to_all(x, axis, split_axis=0, concat_axis=0, tiled=True)  4.5 us
  transfers between devices with their start and end apart: 1, of which 1 were waited for; matrix products, arithmetic and copies ran while one was open for 1% of the time, Pallas kernels for 0%

profile of v8, /device:TPU:1, one launch (start us, length us, event | category | flops | bytes accessed | tf_op | source)
XLA Modules:
  0.0 105.5 jit_solution(1000016802020168846)
XLA Ops:
  0.6 10.4 %all-to-all-start = ((s32[32,1,64]{2,1,0:T(1,128)}), s32[32,1,64]{2,1,0:T(1,128)S(1)}, u32[]{:S(2)}, u32[]{:S(2)}) async-start(s32[32,1,64]{2,1,0:T(1,128)} %bitcast.17), calls=%async_computation | async-start | bytes 32768 | tf_op jit(solution)/shard_map/all_to_all | solution.py:240
  11.0 0.0 copy-start.6
  11.0 0.9 pad_maximum_fusion.both_ref
  12.0 0.0 copy-done.6
  12.0 0.0 copy-start
  12.0 1.1 %copy-done = bf16[512,768]{1,0:T(8,128)(2,1)S(1)} copy-done((bf16[512,768]{1,0:T(8,128)(2,1)S(1)}, bf16[512,768]{1,0:T(8,128)(2,1)}, u32[]{:S(2)}) %copy-start) | copy-done | bytes 786456
  13.1 0.4 shard_map.120.table_ref
  13.5 4.5 %all-to-all-done = s32[32,1,64]{2,1,0:T(1,128)S(1)} async-done(((s32[32,1,64]{2,1,0:T(1,128)}), s32[32,1,64]{2,1,0:T(1,128)S(1)}, u32[]{:S(2)}, u32[]{:S(2)}) %all-to-all-start) | async-done | bytes 8224 | tf_op jit(solution)/shard_map/all_to_all | solution.py:240
  18.0 0.7 shard_map.121
  18.7 0.0 copy-start.2
  18.7 0.0 copy-start.3
  18.7 0.0 copy-start.4
  18.7 0.0 copy-start.5
  18.7 15.8 %all_to_all.36.got_ref = bf16[32,17,4,128]{3,2,1,0:T(4,128)(2,1)S(1)} all-to-all(bf16[32,17,4,128]{3,2,1,0:T(4,128)(2,1)S(1)} %shard_map.121), channel_id=1, replica_groups=mesh['batch'=16,'item'=32] {'item'}, dimensions={0} | all-to-all | bytes 1114112 | tf_op jit(solution)/shard_map/all_to_all | solution.py:240
  34.5 0.0 copy-done.2
  34.5 0.0 copy-done.4
  34.5 4.9 %shard_map.122 = (bf16[32,17,4,128]{3,2,1,0:T(4,128)(2,1)S(1)}, f32[256,128]{1,0:T(8,128)}) custom-call(bf16[32,17,4,128]{3,2,1,0:T(4,128)(2,1)S(1)} %all_to_all.36.got_ref, bf16[256,128]{1,0:T(8,128)(2,1)S(1)} %copy-done.2, s32[16,128]{1,0:T(8,128)S(1)} %bitcast.12, s32[16,128]{1,0:T(8,128)S(1)} %bitcast.13, s32[16,128]{1,0:T(8,128)S(1)} %bitcast.14), custom_call_target="tpu_custom_call" | custom-call | flops 3623878656 | tf_op jit(solution)/shard_map/pallas_call | solution.py:225
  39.4 0.0 copy-start.1
  39.5 15.5 %all_to_all.37.back_ref = bf16[32,17,4,128]{3,2,1,0:T(4,128)(2,1)S(1)} all-to-all(bf16[32,17,4,128]{3,2,1,0:T(4,128)(2,1)S(1)} %get-tuple-element.12), channel_id=1, replica_groups=mesh['batch'=16,'item'=32] {'item'}, dimensions={0} | all-to-all | bytes 1114112 | tf_op jit(solution)/shard_map/all_to_all | solution.py:240
  55.0 1.1 %shard_map.123 = (f32[64,512]{1,0:T(8,128)S(1)}, f32[1,512]{1,0:T(1,128)S(1)}, f32[32,4,384]{2,1,0:T(4,128)S(1)}) custom-call(bf16[32,17,4,128]{3,2,1,0:T(4,128)(2,1)S(1)} %all_to_all.37.back_ref, s32[32,64]{1,0:T(8,128)S(1)} %bitcast.11, bf16[512,768]{1,0:T(8,128)(2,1)S(1)} %copy-done.1), custom_call_target="tpu_custom_call" | custom-call | flops 301989888 | tf_op jit(solution)/shard_map/pallas_call | solution.py:225
  56.1 11.8 %all_to_all.38.in_ref = f32[32,4,384]{2,1,0:T(4,128)S(1)} all-to-all(f32[32,4,384]{2,1,0:T(4,128)S(1)} %get-tuple-element.13), channel_id=1, replica_groups=mesh['batch'=16,'item'=32] {'item'}, dimensions={0} | all-to-all | bytes 393216 | tf_op jit(solution)/shard_map/all_to_all | solution.py:240
  68.0 24.4 %all_to_all.39.in_ref = bf16[16,4,384]{2,1,0:T(4,128)(2,1)S(1)} all-to-all(bf16[16,4,384]{2,1,0:T(4,128)(2,1)S(1)} %shard_map.124), channel_id=1, replica_groups=mesh['batch'=16,'item'=32] {'batch'}, dimensions={0} | all-to-all | bytes 98304 | tf_op jit(solution)/shard_map/all_to_all | solution.py:240
  92.4 12.4 %all_to_all.40.in_ref = bf16[32,4,384]{2,1,0:T(4,128)(2,1)S(1)} all-to-all(bf16[32,4,384]{2,1,0:T(4,128)(2,1)S(1)} %shard_map.125), channel_id=1, replica_groups=mesh['batch'=16,'item'=32] {'item'}, dimensions={0} | all-to-all | bytes 196608 | tf_op jit(solution)/shard_map/all_to_all | solution.py:240
  104.8 0.8 shard_map.126
  (6 shorter events, 0.1 us)
Async XLA Ops:
  0.6 17.4 %all-to-all-start = ((s32[32,1,64]{2,1,0:T(1,128)}), s32[32,1,64]{2,1,0:T(1,128)S(1)}, u32[]{:S(2)}, u32[]{:S(2)}) async-start(s32[32,1,64]{2,1,0:T(1,128)} %bitcast.17), calls=%async_computation | async-start | bytes 32768 | tf_op jit(solution)/shard_map/all_to_all | solution.py:240
  11.0 1.0 copy-start.6
  12.0 1.1 %copy-start = (bf16[512,768]{1,0:T(8,128)(2,1)S(1)}, bf16[512,768]{1,0:T(8,128)(2,1)}, u32[]{:S(2)}) copy-start(bf16[512,768]{1,0:T(8,128)(2,1)} %feat_ref.3) | copy-start | bytes 2359300
  18.7 15.8 %copy-start.2 = (bf16[256,128]{1,0:T(8,128)(2,1)S(1)}, bf16[256,128]{1,0:T(8,128)(2,1)}, u32[]{:S(2)}) copy-start(bf16[256,128]{1,0:T(8,128)(2,1)} %user_ref.1) | copy-start | bytes 196612
  18.7 15.8 %copy-start.3 = (s32[2048]{0:T(1024)S(1)}, s32[2048]{0:T(1024)}, u32[]{:S(2)}) copy-start(s32[2048]{0:T(1024)} %param.14) | copy-start | bytes 24580
  18.7 15.8 %copy-start.4 = (s32[2048]{0:T(1024)S(1)}, s32[2048]{0:T(1024)}, u32[]{:S(2)}) copy-start(s32[2048]{0:T(1024)} %param.16) | copy-start | bytes 24580
  18.7 15.8 %copy-start.5 = (s32[2048]{0:T(1024)S(1)}, s32[2048]{0:T(1024)}, u32[]{:S(2)}) copy-start(s32[2048]{0:T(1024)} %param.17) | copy-start | bytes 24580
  39.4 15.5 %copy-start.1 = (bf16[512,768]{1,0:T(8,128)(2,1)S(1)}, bf16[512,768]{1,0:T(8,128)(2,1)}, u32[]{:S(2)}) copy-start(bf16[512,768]{1,0:T(8,128)(2,1)} %feat_ref.3) | copy-start | bytes 2359300
